TPU v7x, 32 devices: a whole 2x2x4 slice. The times are simulated.
32 devices in a mesh: ep: 8 (over z, x), tp: 4 (over y, core).
Axes of the slice: x: 2, y: 2, z: 4, core: 2. Of those that a mesh axis runs over, the one named last changes fastest.
Arguments:
- inputs: bfloat16 [2, 512, 2, 2048], P(None, 'ep'), may hold values from -6 to 6
- lengths: int32 [2, 2], replicated, may hold values from 128 to 512, as said below
- routes: int32 [2, 512, 2, 8], P(None, 'ep'), may hold values from 0 to 15, all different within a row; in each aligned block of 128 rows (0 to 127, 128 to 255, ..., all dimensions but the last counted through in order) at most 80 rows name the same one
- w_query: bfloat16 [2048, 2048], P('ep', 'tp'), may hold values from -0.125 to 0.125
- w_key: bfloat16 [2048, 2048], P('ep', 'tp'), may hold values from -0.125 to 0.125
- w_value: bfloat16 [2048, 2048], P('ep', 'tp'), may hold values from -0.125 to 0.125
- w_output: bfloat16 [2048, 2048], P('ep', 'tp'), may hold values from -3 to 3
- w_router: bfloat16 [2048, 16], P('ep'), may hold values from -0.0625 to 0.0625
- attn_gain: bfloat16 [2048], P('ep'), may hold values from 0.5 to 1.5
- moe_gain: bfloat16 [2048], P('ep'), may hold values from 0.5 to 1.5
- query_gain: bfloat16 [2048], P('ep'), may hold values from 0.5 to 1.5
- key_gain: bfloat16 [2048], P('ep'), may hold values from 0.5 to 1.5
- w_gate: bfloat16 [16, 2048, 1024], P('ep', None, 'tp'), may hold values from -0.125 to 0.125
- w_up: bfloat16 [16, 2048, 1024], P('ep', None, 'tp'), may hold values from -0.125 to 0.125
- w_down: bfloat16 [16, 1024, 2048], P('ep', 'tp'), may hold values from -4 to 4
- out_grad: bfloat16 [2, 512, 2, 2048], P(None, 'ep'), may hold values from -6 to 6
Outputs:
- out: bfloat16 [2, 512, 2, 2048], P(None, 'ep')
- input_grad: float32 [2, 512, 2, 2048], P(None, 'ep')
- grad_query: float32 [2048, 2048], P('ep', 'tp')
- grad_key: float32 [2048, 2048], P('ep', 'tp')
- grad_value: float32 [2048, 2048], P('ep', 'tp')
- grad_output: float32 [2048, 2048], P('ep', 'tp')
- grad_router: float32 [2048, 16], P('ep')
- grad_attn_gain: float32 [2048], P('ep')
- grad_moe_gain: float32 [2048], P('ep')
- grad_query_gain: float32 [2048], P('ep')
- grad_key_gain: float32 [2048], P('ep')
- grad_gate: float32 [16, 2048, 1024], P('ep', None, 'tp')
- grad_up: float32 [16, 2048, 1024], P('ep', None, 'tp')
- grad_down: float32 [16, 1024, 2048], P('ep', 'tp')
Inputs may be any that keep to these rules, and one draw needn't show every extreme that they name: `lengths`: in each micro-batch one sequence, which one drawn from the seed, has all 512 slots valid. `routes`: A row names 8 different experts. In each aligned block of 128 rows (the rows of one device in one micro-batch, in the array's order) no expert is named by more than 80 rows, and in some block some expert by exactly 80.
All inputs are finite; a program needn't handle non-finite values.
Results may differ from a plain program's by a relative error of at most 0.024.
Values may be sent and summed in bfloat16 or wider, within the bound.
A program may use at most 320 MiB of HBM per device.

v0:
```python
import jax
import jax.numpy as jnp
from jax import lax
from jax.sharding import PartitionSpec as P

HEAD_DIM = 128


EPSILON = 1e-05
THETA_BASE = 10000.0
NEGATIVE = -1e30


def row_scale(values):
    return lax.rsqrt(jnp.mean(values * values, axis=-1, keepdims=True) + EPSILON)


def turn_half(values):
    half_width = values.shape[-1] // 2
    return jnp.concatenate([-values[..., half_width:], values[..., :half_width]], axis=-1)


def rope_tables(first_place, place_count):
    half_width = HEAD_DIM // 2
    places = (first_place + jnp.arange(place_count, dtype=jnp.int32)).astype(jnp.float32)
    inverse = THETA_BASE ** (-jnp.arange(half_width, dtype=jnp.float32) * 2.0 / HEAD_DIM)
    angles = places[:, None] * inverse[None, :]
    angles = jnp.concatenate([angles, angles], axis=-1)
    return (jnp.cos(angles), jnp.sin(angles))


def rotate_forth(values, cosine_table, sine_table):
    return values * cosine_table + turn_half(values) * sine_table


def rotate_back(values, cosine_table, sine_table):
    return values * cosine_table - turn_half(values) * sine_table


def allowed_table(first_place, query_count, key_count, length):
    query_place = first_place + jnp.arange(query_count, dtype=jnp.int32)
    key_place = jnp.arange(key_count, dtype=jnp.int32)
    return (key_place[None, :] <= query_place[:, None]) & (key_place[None, :] < length)


def attend_forward(queries, key_rows, value_rows, first_place, length, score_scale):
    allowed = allowed_table(first_place, queries.shape[0], key_rows.shape[0], length)
    scores = (
        jnp.einsum("chd,lhd->hcl", queries, key_rows, preferred_element_type=jnp.float32)
        * score_scale
    )
    scores = jnp.where(allowed[None], scores, NEGATIVE)
    highest = jnp.max(scores, axis=-1, keepdims=True)
    weights = jnp.exp(scores - highest)
    totals = jnp.sum(weights, axis=-1, keepdims=True)
    probability = (weights / totals).astype(jnp.bfloat16)
    attended = jnp.einsum(
        "hcl,lhd->chd", probability, value_rows, preferred_element_type=jnp.float32
    )
    return (attended, (highest + jnp.log(totals))[..., 0])


def attend_backward(
    queries, key_rows, value_rows, attended_grad, log_total, first_place, length, score_scale
):
    allowed = allowed_table(first_place, queries.shape[0], key_rows.shape[0], length)
    scores = (
        jnp.einsum("chd,lhd->hcl", queries, key_rows, preferred_element_type=jnp.float32)
        * score_scale
    )
    scores = jnp.where(allowed[None], scores, NEGATIVE)
    probability = jnp.exp(scores - log_total[..., None])
    prob_grad = jnp.einsum(
        "chd,lhd->hcl", attended_grad, value_rows, preferred_element_type=jnp.float32
    )
    centre = jnp.sum(probability * prob_grad, axis=-1, keepdims=True)
    score_grad = (probability * (prob_grad - centre)).astype(jnp.bfloat16)
    query_grad = (
        jnp.einsum("hcl,lhd->chd", score_grad, key_rows, preferred_element_type=jnp.float32)
        * score_scale
    )
    key_grad = (
        jnp.einsum("hcl,chd->lhd", score_grad, queries, preferred_element_type=jnp.float32)
        * score_scale
    )
    value_grad = jnp.einsum(
        "hcl,chd->lhd",
        probability.astype(jnp.bfloat16),
        attended_grad,
        preferred_element_type=jnp.float32,
    )
    return (query_grad, key_grad, value_grad, centre[..., 0])


def gather_keys(key_blocks, value_blocks):
    return (
        lax.all_gather(key_blocks, "ep", axis=0, tiled=True),
        lax.all_gather(value_blocks, "ep", axis=0, tiled=True),
    )


def contract_rows(left, right):
    return lax.dot_general(
        left, right, (((0,), (0,)), ((), ())), preferred_element_type=jnp.float32
    )


def contract_cols(left, right):
    return lax.dot_general(
        left, right, (((1,), (1,)), ((), ())), preferred_element_type=jnp.float32
    )


def shards(
    inputs,
    lengths,
    routes,
    w_query,
    w_key,
    w_value,
    w_output,
    w_router,
    attn_gain,
    moe_gain,
    query_gain,
    key_gain,
    w_gate,
    w_up,
    w_down,
    out_grad,
):
    micro_count, block_rows, sequence_count, width = inputs.shape
    axis_devices = lax.axis_size("ep")
    shard_index = lax.axis_index("ep")
    hidden_index = lax.axis_index("tp")
    local_width = w_query.shape[1]
    local_heads = local_width // HEAD_DIM
    local_experts = w_gate.shape[0]
    expert_count = local_experts * axis_devices
    top_count = routes.shape[-1]
    row_count = block_rows * sequence_count
    sequence_length = block_rows * axis_devices
    capacity = 5 * row_count * top_count // (4 * expert_count)
    score_scale = HEAD_DIM ** (-0.5)
    first_place = shard_index * block_rows
    cosine_table, sine_table = rope_tables(first_place, block_rows)
    cosine_table = cosine_table[:, None, None, :]
    sine_table = sine_table[:, None, None, :]
    local_place = first_place + jnp.arange(block_rows, dtype=jnp.int32)
    expert_numbers = jnp.arange(expert_count, dtype=jnp.int32)
    zero_width = jnp.zeros((width,), jnp.float32)
    head_shape = (block_rows, sequence_count, local_heads, HEAD_DIM)
    grad_query = jnp.zeros((width, local_width), jnp.float32)
    grad_key = jnp.zeros((width, local_width), jnp.float32)
    grad_value = jnp.zeros((width, local_width), jnp.float32)
    grad_output = jnp.zeros((width, local_width), jnp.float32)
    grad_router = jnp.zeros((width, expert_count), jnp.float32)
    grad_gain_attn = zero_width
    grad_gain_moe = zero_width
    grad_gain_query = zero_width
    grad_gain_key = zero_width
    grad_gate = jnp.zeros(w_gate.shape, jnp.float32)
    grad_up = jnp.zeros(w_up.shape, jnp.float32)
    grad_down = jnp.zeros(w_down.shape, jnp.float32)
    outputs_list = []
    input_grads = []
    for micro_index in range(micro_count):
        gathered = (
            lax.all_gather(w_query, "ep", axis=0, tiled=True),
            lax.all_gather(w_key, "ep", axis=0, tiled=True),
            lax.all_gather(w_value, "ep", axis=0, tiled=True),
            lax.all_gather(w_output, "ep", axis=0, tiled=True),
            lax.all_gather(w_router, "ep", axis=0, tiled=True),
            lax.all_gather(attn_gain, "ep", axis=0, tiled=True),
            lax.all_gather(moe_gain, "ep", axis=0, tiled=True),
            lax.all_gather(query_gain, "ep", axis=0, tiled=True),
            lax.all_gather(key_gain, "ep", axis=0, tiled=True),
        )
        full_query, full_key, full_value, full_output, full_router = (
            gathered[0],
            gathered[1],
            gathered[2],
            gathered[3],
            gathered[4],
        )
        gain_attn = gathered[5].astype(jnp.float32)
        gain_moe = gathered[6].astype(jnp.float32)
        gain_query = lax.dynamic_slice_in_dim(
            gathered[7].astype(jnp.float32), hidden_index * local_width, local_width
        )
        gain_key = lax.dynamic_slice_in_dim(
            gathered[8].astype(jnp.float32), hidden_index * local_width, local_width
        )
        hidden_in = inputs[micro_index].reshape(row_count, width).astype(jnp.float32)
        scale_in = row_scale(hidden_in)
        normed_in = (hidden_in * scale_in * gain_attn).astype(jnp.bfloat16)
        query_pre = jnp.dot(normed_in, full_query, preferred_element_type=jnp.float32)
        key_pre = jnp.dot(normed_in, full_key, preferred_element_type=jnp.float32)
        value_rows = jnp.dot(normed_in, full_value, preferred_element_type=jnp.float32).astype(
            jnp.bfloat16
        )
        query_square, key_square = lax.psum(
            (jnp.sum(query_pre * query_pre, axis=1), jnp.sum(key_pre * key_pre, axis=1)), "tp"
        )
        query_scale = lax.rsqrt(query_square / width + EPSILON)[:, None]
        key_scale = lax.rsqrt(key_square / width + EPSILON)[:, None]
        query_turned = rotate_forth(
            (query_pre * query_scale * gain_query).reshape(head_shape), cosine_table, sine_table
        ).astype(jnp.bfloat16)
        key_turned = rotate_forth(
            (key_pre * key_scale * gain_key).reshape(head_shape), cosine_table, sine_table
        ).astype(jnp.bfloat16)
        key_blocks = key_turned.reshape(block_rows, sequence_count, local_width)
        value_blocks = value_rows.reshape(block_rows, sequence_count, local_width)
        key_all, value_all = gather_keys(key_blocks, value_blocks)
        attended_list = []
        log_totals = []
        for sequence in range(sequence_count):
            attended_one, log_one = attend_forward(
                query_turned[:, sequence],
                key_all[:, sequence].reshape(sequence_length, local_heads, HEAD_DIM),
                value_all[:, sequence].reshape(sequence_length, local_heads, HEAD_DIM),
                first_place,
                lengths[micro_index, sequence],
                score_scale,
            )
            attended_list.append(attended_one)
            log_totals.append(log_one)
        attended = (
            jnp.stack(attended_list, axis=1).reshape(row_count, local_width).astype(jnp.bfloat16)
        )
        attn_rows = lax.psum(contract_cols(attended, full_output), "tp")
        middle = hidden_in + attn_rows
        scale_mid = row_scale(middle)
        normed_mid = (middle * scale_mid * gain_moe).astype(jnp.bfloat16)
        logits = jnp.dot(normed_mid, full_router, preferred_element_type=jnp.float32)
        probs = jax.nn.softmax(logits, axis=-1)
        named_rows = routes[micro_index].reshape(row_count, top_count)
        picked = named_rows[:, :, None] == expert_numbers[None, None, :]
        picked_float = picked.astype(jnp.float32)
        gates = jnp.sum(picked_float * probs[:, None, :], axis=-1)
        flat_pick = picked.reshape(row_count * top_count, expert_count).astype(jnp.int32)
        places = jnp.sum((jnp.cumsum(flat_pick, axis=0) - 1) * flat_pick, axis=1)
        slots = named_rows.reshape(-1) * capacity + places
        outgoing = (
            jnp.zeros((expert_count * capacity, width), jnp.bfloat16)
            .at[slots]
            .set(jnp.repeat(normed_mid, top_count, axis=0))
        )
        arrived = lax.all_to_all(
            outgoing.reshape(axis_devices, local_experts, capacity, width),
            "ep",
            split_axis=0,
            concat_axis=0,
            tiled=True,
        )
        gate_in = jnp.einsum("secd,edf->secf", arrived, w_gate, preferred_element_type=jnp.float32)
        up_in = jnp.einsum("secd,edf->secf", arrived, w_up, preferred_element_type=jnp.float32)
        active = jax.nn.silu(gate_in)
        inner = (active * up_in).astype(jnp.bfloat16)
        partial_out = jnp.einsum(
            "secf,efd->secd", inner, w_down, preferred_element_type=jnp.float32
        ).astype(jnp.bfloat16)
        returned = lax.all_to_all(
            partial_out, "ep", split_axis=0, concat_axis=0, tiled=True
        ).reshape(expert_count * capacity, width)
        picked_rows = returned[slots].reshape(row_count, top_count, width)
        moe_part = jnp.sum(gates[:, :, None] * picked_rows.astype(jnp.float32), axis=1)
        moe_rows = lax.psum(moe_part.astype(jnp.bfloat16), "tp").astype(jnp.float32)
        valid = (
            (local_place[:, None] < lengths[micro_index][None, :])
            .astype(jnp.float32)
            .reshape(row_count)
        )
        outputs_list.append(
            ((middle + moe_rows) * valid[:, None])
            .astype(jnp.bfloat16)
            .reshape(block_rows, sequence_count, width)
        )
        grad_rows = (
            out_grad[micro_index].reshape(row_count, width).astype(jnp.float32) * valid[:, None]
        )
        grad_pieces = (
            (gates[:, :, None] * grad_rows[:, None, :])
            .astype(jnp.bfloat16)
            .reshape(row_count * top_count, width)
        )
        grad_out = (
            jnp.zeros((expert_count * capacity, width), jnp.bfloat16).at[slots].set(grad_pieces)
        )
        grad_arrived = lax.all_to_all(
            grad_out.reshape(axis_devices, local_experts, capacity, width),
            "ep",
            split_axis=0,
            concat_axis=0,
            tiled=True,
        )
        inner_grad = jnp.einsum(
            "secd,efd->secf", grad_arrived, w_down, preferred_element_type=jnp.float32
        )
        sigmoid_gate = jax.nn.sigmoid(gate_in)
        gate_in_grad = (
            inner_grad * up_in * sigmoid_gate * (1.0 + gate_in * (1.0 - sigmoid_gate))
        ).astype(jnp.bfloat16)
        up_in_grad = (inner_grad * active).astype(jnp.bfloat16)
        grad_gate = grad_gate + jnp.einsum(
            "secd,secf->edf", arrived, gate_in_grad, preferred_element_type=jnp.float32
        )
        grad_up = grad_up + jnp.einsum(
            "secd,secf->edf", arrived, up_in_grad, preferred_element_type=jnp.float32
        )
        grad_down = grad_down + jnp.einsum(
            "secf,secd->efd", inner, grad_arrived, preferred_element_type=jnp.float32
        )
        expert_grad = jnp.einsum(
            "secf,edf->secd", gate_in_grad, w_gate, preferred_element_type=jnp.float32
        )
        expert_grad = expert_grad + jnp.einsum(
            "secf,edf->secd", up_in_grad, w_up, preferred_element_type=jnp.float32
        )
        grad_back = lax.all_to_all(
            expert_grad, "ep", split_axis=0, concat_axis=0, tiled=True
        ).reshape(expert_count * capacity, width)
        moe_in_part = jnp.sum(grad_back[slots].reshape(row_count, top_count, width), axis=1)
        gate_part = jnp.sum(grad_rows[:, None, :] * picked_rows.astype(jnp.float32), axis=-1)
        moe_in_grad, gate_grad_rows = lax.psum((moe_in_part, gate_part), "tp")
        prob_grad = jnp.sum(picked_float * gate_grad_rows[:, :, None], axis=1)
        logit_grad = (
            probs * (prob_grad - jnp.sum(probs * prob_grad, axis=1, keepdims=True))
        ).astype(jnp.bfloat16)
        grad_router = grad_router + contract_rows(normed_mid, logit_grad)
        normed_mid_grad = moe_in_grad + contract_cols(logit_grad, full_router)
        grad_gain_moe = grad_gain_moe + jnp.sum(normed_mid_grad * middle * scale_mid, axis=0)
        scaled_mid = gain_moe * normed_mid_grad
        middle_grad = (
            grad_rows
            + scale_mid * scaled_mid
            - middle * scale_mid**3 * jnp.mean(scaled_mid * middle, axis=1, keepdims=True)
        )
        middle_low = middle_grad.astype(jnp.bfloat16)
        grad_output = grad_output + contract_rows(middle_low, attended)
        attended_grad = (
            jnp.dot(middle_low, full_output, preferred_element_type=jnp.float32)
            .astype(jnp.bfloat16)
            .reshape(head_shape)
        )
        key_back, value_back = gather_keys(key_blocks, value_blocks)
        query_grads = []
        key_grads = []
        value_grads = []
        centres = []
        for sequence in range(sequence_count):
            query_one, key_one, value_one, centre_one = attend_backward(
                query_turned[:, sequence],
                key_back[:, sequence].reshape(sequence_length, local_heads, HEAD_DIM),
                value_back[:, sequence].reshape(sequence_length, local_heads, HEAD_DIM),
                attended_grad[:, sequence],
                log_totals[sequence],
                first_place,
                lengths[micro_index, sequence],
                score_scale,
            )
            query_grads.append(query_one)
            key_grads.append(key_one)
            value_grads.append(value_one)
            centres.append(centre_one)
        key_grad_all = jnp.stack(key_grads, axis=1).reshape(
            sequence_length, sequence_count, local_width
        )
        value_grad_all = jnp.stack(value_grads, axis=1).reshape(
            sequence_length, sequence_count, local_width
        )
        key_grad, value_grad = (
            lax.psum_scatter(
                key_grad_all.astype(jnp.bfloat16), "ep", scatter_dimension=0, tiled=True
            ).astype(jnp.float32),
            lax.psum_scatter(
                value_grad_all.astype(jnp.bfloat16), "ep", scatter_dimension=0, tiled=True
            ).astype(jnp.float32),
        )
        value_grad_low = value_grad.reshape(row_count, local_width).astype(jnp.bfloat16)
        query_norm_grad = rotate_back(
            jnp.stack(query_grads, axis=1), cosine_table, sine_table
        ).reshape(row_count, local_width)
        key_norm_grad = rotate_back(key_grad.reshape(head_shape), cosine_table, sine_table).reshape(
            row_count, local_width
        )
        query_inner, key_inner = lax.psum(
            (
                jnp.sum(gain_query * query_norm_grad * query_pre, axis=1),
                jnp.sum(gain_key * key_norm_grad * key_pre, axis=1),
            ),
            "tp",
        )
        query_pre_grad = (
            query_scale * gain_query * query_norm_grad
            - query_pre * query_scale**3 * query_inner[:, None] / width
        ).astype(jnp.bfloat16)
        key_pre_grad = (
            key_scale * gain_key * key_norm_grad
            - key_pre * key_scale**3 * key_inner[:, None] / width
        ).astype(jnp.bfloat16)
        query_gain_piece = jnp.sum(query_norm_grad * query_pre * query_scale, axis=0)
        key_gain_piece = jnp.sum(key_norm_grad * key_pre * key_scale, axis=0)
        grad_query = grad_query + contract_rows(normed_in, query_pre_grad)
        grad_key = grad_key + contract_rows(normed_in, key_pre_grad)
        grad_value = grad_value + contract_rows(normed_in, value_grad_low)
        input_part = (
            contract_cols(query_pre_grad, full_query)
            + contract_cols(key_pre_grad, full_key)
            + contract_cols(value_grad_low, full_value)
        )
        query_gain_full = lax.dynamic_update_slice(
            zero_width, query_gain_piece, (hidden_index * local_width,)
        )
        key_gain_full = lax.dynamic_update_slice(
            zero_width, key_gain_piece, (hidden_index * local_width,)
        )
        normed_in_grad, query_gain_sum, key_gain_sum = (
            lax.psum(input_part.astype(jnp.bfloat16), "tp").astype(jnp.float32),
            lax.psum(query_gain_full.astype(jnp.bfloat16), "tp").astype(jnp.float32),
            lax.psum(key_gain_full.astype(jnp.bfloat16), "tp").astype(jnp.float32),
        )
        grad_gain_query = grad_gain_query + query_gain_sum
        grad_gain_key = grad_gain_key + key_gain_sum
        grad_gain_attn = grad_gain_attn + jnp.sum(normed_in_grad * hidden_in * scale_in, axis=0)
        scaled_in = gain_attn * normed_in_grad
        hidden_grad = (
            middle_grad
            + scale_in * scaled_in
            - hidden_in * scale_in**3 * jnp.mean(scaled_in * hidden_in, axis=1, keepdims=True)
        )
        input_grads.append(hidden_grad.reshape(block_rows, sequence_count, width))
    summed = (
        lax.psum_scatter(
            grad_query.astype(jnp.bfloat16), "ep", scatter_dimension=0, tiled=True
        ).astype(jnp.float32),
        lax.psum_scatter(
            grad_key.astype(jnp.bfloat16), "ep", scatter_dimension=0, tiled=True
        ).astype(jnp.float32),
        lax.psum_scatter(
            grad_value.astype(jnp.bfloat16), "ep", scatter_dimension=0, tiled=True
        ).astype(jnp.float32),
        lax.psum_scatter(
            grad_output.astype(jnp.bfloat16), "ep", scatter_dimension=0, tiled=True
        ).astype(jnp.float32),
        lax.psum_scatter(
            grad_router.astype(jnp.bfloat16), "ep", scatter_dimension=0, tiled=True
        ).astype(jnp.float32),
        lax.psum_scatter(
            grad_gain_attn.astype(jnp.bfloat16), "ep", scatter_dimension=0, tiled=True
        ).astype(jnp.float32),
        lax.psum_scatter(
            grad_gain_moe.astype(jnp.bfloat16), "ep", scatter_dimension=0, tiled=True
        ).astype(jnp.float32),
        lax.psum_scatter(
            grad_gain_query.astype(jnp.bfloat16), "ep", scatter_dimension=0, tiled=True
        ).astype(jnp.float32),
        lax.psum_scatter(
            grad_gain_key.astype(jnp.bfloat16), "ep", scatter_dimension=0, tiled=True
        ).astype(jnp.float32),
    )
    return (
        jnp.stack(outputs_list, axis=0),
        jnp.stack(input_grads, axis=0),
        summed[0],
        summed[1],
        summed[2],
        summed[3],
        summed[4],
        summed[5],
        summed[6],
        summed[7],
        summed[8],
        grad_gate,
        grad_up,
        grad_down,
    )


def solution(mesh):
    return jax.shard_map(
        shards,
        mesh=mesh,
        in_specs=(
            P(None, "ep", None, None),
            P(),
            P(None, "ep", None, None),
            P("ep", "tp"),
            P("ep", "tp"),
            P("ep", "tp"),
            P("ep", "tp"),
            P("ep", None),
            P("ep"),
            P("ep"),
            P("ep"),
            P("ep"),
            P("ep", None, "tp"),
            P("ep", None, "tp"),
            P("ep", "tp", None),
            P(None, "ep", None, None),
        ),
        out_specs=(
            P(None, "ep", None, None),
            P(None, "ep", None, None),
            P("ep", "tp"),
            P("ep", "tp"),
            P("ep", "tp"),
            P("ep", "tp"),
            P("ep", None),
            P("ep"),
            P("ep"),
            P("ep"),
            P("ep"),
            P("ep", None, "tp"),
            P("ep", None, "tp"),
            P("ep", "tp", None),
        ),
        check_vma=False,
    )
```

profile of v0, /device:TPU:1, one launch (start us, length us, event | category | flops | bytes accessed | tf_op | source)
XLA Modules:
  0.0 2367.2 jit_solution(17185521742022245811)
XLA Ops:
  11.3 17.9 all-gather.2
  29.2 12.8 all-gather
  62.8 47.7 %all-gather.19.cloned.1.call-done = bf16[2048,512]{1,0:T(8,128)(2,1)} async-done(((bf16[256,512]{1,0:T(8,128)(2,1)}), bf16[2048,512]{1,0:T(8,128)(2,1)}) %all-gather.19.cloned.1.call-update) | async-done | bytes 2097168 | tf_op jit(solution)/shard_map/all_gather | solution.py:170
  148.1 12.4 all-gather.13.cloned.1.call-done
  172.8 15.3 all-gather.1
  188.2 12.9 all-gather.3
  207.7 25.2 %all_gather.62 = bf16[2048,16]{0,1:T(8,128)(2,1)S(1)} all-gather(bf16[256,16]{0,1:T(8,128)(2,1)} %param.23), channel_id=1, replica_groups=mesh['ep'=8,'tp'=4] {'ep'}, dimensions={0}, use_global_device_ids=true | all-gather | bytes 73728 | tf_op jit(solution)/shard_map/all_gather | solution.py:173
  302.2 22.9 all-gather.15.cloned.1.call-done
  341.6 33.8 %all-gather.23.cloned.1.call-done = bf16[2048,512]{1,0:T(8,128)(2,1)} async-done(((bf16[256,512]{1,0:T(8,128)(2,1)}), bf16[2048,512]{1,0:T(8,128)(2,1)}) %all-gather.23.cloned.1.call-update) | async-done | bytes 2097168 | tf_op jit(solution)/shard_map/all_gather | solution.py:172
  383.2 48.7 %all-reduce.22.cloned.1.call-done = (f32[128,2048]{1,0:T(8,128)}, f32[128,2048]{1,0:T(8,128)}) async-done(((f32[128,2048]{1,0:T(8,128)}, f32[128,2048]{1,0:T(8,128)}), (f32[128,2048]{1,0:T(8,128)}, f32[128,2048]{1,0:T(8,128)})) %all-reduce.22.cloned.1.call-update) | async-done | bytes 2097168 | tf_op jit(solution)/shard_map/psum | solution.py:232
  463.8 105.2 %all-to-all-done.4 = bf16[8,2,80,2048]{3,2,1,0:T(8,128)(2,1)} async-done(((bf16[8,2,80,2048]{3,2,1,0:T(8,128)(2,1)}), bf16[8,2,80,2048]{3,2,1,0:T(8,128)(2,1)}, u32[]{:S(2)}, u32[]{:S(2)}) %all-to-all-start.4) | async-done | bytes 5242912 | tf_op jit(solution)/shard_map/all_to_all | solution.py:291
  596.1 92.1 %all-to-all-done = bf16[8,2,80,2048]{3,2,1,0:T(8,128)(2,1)} async-done(((bf16[8,2,80,2048]{3,2,1,0:T(8,128)(2,1)}), bf16[8,2,80,2048]{3,2,1,0:T(8,128)(2,1)}, u32[]{:S(2)}, u32[]{:S(2)}) %all-to-all-start) | async-done | bytes 5242912 | tf_op jit(solution)/shard_map/all_to_all | solution.py:250
  703.8 104.5 %all-to-all-done.6 = bf16[8,2,80,2048]{3,2,1,0:T(8,128)(2,1)} async-done(((bf16[8,2,80,2048]{3,2,1,0:T(8,128)(2,1)}), bf16[8,2,80,2048]{3,2,1,0:T(8,128)(2,1)}, u32[]{:S(2)}, u32[]{:S(2)}) %all-to-all-start.6) | async-done | bytes 5242912 | tf_op jit(solution)/shard_map/all_to_all | solution.py:291
  833.7 94.6 %all-to-all-done.2 = bf16[8,2,80,2048]{3,2,1,0:T(8,128)(2,1)} async-done(((bf16[8,2,80,2048]{3,2,1,0:T(8,128)(2,1)}), bf16[8,2,80,2048]{3,2,1,0:T(8,128)(2,1)}, u32[]{:S(2)}, u32[]{:S(2)}) %all-to-all-start.2) | async-done | bytes 5242912 | tf_op jit(solution)/shard_map/all_to_all | solution.py:250
  953.4 94.6 %all-to-all-done.1 = bf16[8,2,80,2048]{3,2,1,0:T(8,128)(2,1)} async-done(((bf16[8,2,80,2048]{3,2,1,0:T(8,128)(2,1)}), bf16[8,2,80,2048]{3,2,1,0:T(8,128)(2,1)}, u32[]{:S(2)}, u32[]{:S(2)}) %all-to-all-start.1) | async-done | bytes 5242912 | tf_op jit(solution)/shard_map/all_to_all | solution.py:264
  1062.5 105.1 %all-to-all-done.3 = bf16[8,2,80,2048]{3,2,1,0:T(8,128)(2,1)} async-done(((bf16[8,2,80,2048]{3,2,1,0:T(8,128)(2,1)}), bf16[8,2,80,2048]{3,2,1,0:T(8,128)(2,1)}, u32[]{:S(2)}, u32[]{:S(2)}) %all-to-all-start.3) | async-done | bytes 5242912 | tf_op jit(solution)/shard_map/all_to_all | solution.py:264
  1181.4 217.8 %all-to-all-done.7 = f32[8,2,80,2048]{3,2,1,0:T(8,128)} async-done(((f32[8,2,80,2048]{3,2,1,0:T(8,128)}), f32[8,2,80,2048]{3,2,1,0:T(8,128)}, u32[]{:S(2)}, u32[]{:S(2)}) %all-to-all-start.7) | async-done | bytes 10485792 | tf_op jit(solution)/shard_map/all_to_all | solution.py:321
  1406.8 12.0 gather_fusion
  1418.8 12.1 gather_fusion.1
  1436.6 12.9 gather_fusion.3
  1455.8 176.0 %all-to-all-done.5 = f32[8,2,80,2048]{3,2,1,0:T(8,128)} async-done(((f32[8,2,80,2048]{3,2,1,0:T(8,128)}), f32[8,2,80,2048]{3,2,1,0:T(8,128)}, u32[]{:S(2)}, u32[]{:S(2)}) %all-to-all-start.5) | async-done | bytes 10485792 | tf_op jit(solution)/shard_map/all_to_all | solution.py:321
  1631.8 12.9 gather_fusion.2
  1657.6 16.6 all-reduce.7
  1674.6 31.2 %all-reduce.20.cloned.1.call-done = (f32[128,2048]{1,0:T(8,128)}, f32[128,2048]{1,0:T(8,128)}) async-done(((f32[128,2048]{1,0:T(8,128)}, f32[128,2048]{1,0:T(8,128)}), (f32[128,2048]{1,0:T(8,128)}, f32[128,2048]{1,0:T(8,128)})) %all-reduce.20.cloned.1.call-update) | async-done | bytes 2097168 | tf_op jit(solution)/shard_map/psum | solution.py:326
  1777.4 15.3 reduce-scatter.8.cloned.1.call-done
  1794.7 64.8 %reduce-scatter.10.cloned.1.call-done = bf16[64,2,512]{2,0,1:T(8,128)(2,1)} async-done(((bf16[512,2,512]{2,0,1:T(8,128)(2,1)}), bf16[64,2,512]{2,0,1:T(8,128)(2,1)}) %reduce-scatter.10.cloned.1.call-update) | async-done | bytes 131088 | tf_op jit(solution)/shard_map/reduce_scatter | solution.py:374
  1867.0 98.8 %all-reduce.24.cloned.1.call-done = (bf16[512,2,512]{2,1,0:T(2,128)(2,1)}, bf16[512,2,512]{2,1,0:T(2,128)(2,1)}) async-done(((bf16[512,2,512]{2,1,0:T(2,128)(2,1)}, bf16[512,2,512]{2,1,0:T(2,128)(2,1)}), (bf16[512,2,512]{2,1,0:T(2,128)(2,1)}, bf16[512,2,512]{2,1,0:T(2,128)(2,1)})) %all-reduce.24.cloned.1.call-update) | async-done | bytes 2097168
  2058.6 17.8 all-reduce.26.cloned.1.call-done
  2095.3 30.3 %all-reduce.11 = (bf16[2048]{0:T(1024)(128)(2,1)S(1)}, bf16[2048]{0:T(1024)(128)(2,1)S(1)}, bf16[2048]{0:T(1024)(128)(2,1)S(1)}, bf16[2048]{0:T(1024)(128)(2,1)S(1)}) all-reduce(bf16[2048]{0:T(1024)(128)(2,1)S(1)} %add_convert_fusion.9, bf16[2048]{0:T(1024)(128)(2,1)S(1)} %add_convert_fusion.8, ...), channel_id=11, replica_groups=mesh['ep'=8,'tp'=4] {'ep'}, use_global_device_ids=true, to_apply=%region_83.84.clone | all-reduce | flops 8192 | bytes 32768
  2148.5 68.6 %reduce-scatter.16.cloned.1.call-done = bf16[256,512]{1,0:T(8,128)(2,1)} async-done(((bf16[2048,512]{1,0:T(8,128)(2,1)}), bf16[256,512]{1,0:T(8,128)(2,1)}) %reduce-scatter.16.cloned.1.call-update) | async-done | bytes 262160 | tf_op jit(solution)/shard_map/reduce_scatter | solution.py:441
  2218.9 68.9 %reduce-scatter.14.cloned.1.call-done = bf16[256,512]{1,0:T(8,128)(2,1)} async-done(((bf16[2048,512]{1,0:T(8,128)(2,1)}), bf16[256,512]{1,0:T(8,128)(2,1)}) %reduce-scatter.14.cloned.1.call-update) | async-done | bytes 262160 | tf_op jit(solution)/shard_map/reduce_scatter | solution.py:438
  2289.6 69.0 %reduce-scatter.12.cloned.1.call-done = bf16[256,512]{1,0:T(8,128)(2,1)} async-done(((bf16[2048,512]{1,0:T(8,128)(2,1)}), bf16[256,512]{1,0:T(8,128)(2,1)}) %reduce-scatter.12.cloned.1.call-update) | async-done | bytes 262160 | tf_op jit(solution)/shard_map/reduce_scatter | solution.py:435
  (731 shorter events, 578.7 us)
Async XLA Ops:
  7.2 815.9 %copy-start = (bf16[2,256,2048]{2,1,0:T(8,128)(2,1)S(1)}, bf16[2,256,2048]{2,1,0:T(8,128)(2,1)}, u32[]{:S(2)}) copy-start(bf16[2,256,2048]{2,1,0:T(8,128)(2,1)} %param.30) | copy-start | bytes 6291460
  7.2 53.3 %all-gather.17.cloned.1.call-start = ((), (), s32[]{:S(2)}) async-start(), calls=%async_computation.17 | async-start | bytes 2359296 | tf_op jit(solution)/shard_map/all_gather | solution.py:169
  7.9 102.5 %all-gather.19.cloned.1.call-start = ((), (), s32[]{:S(2)}) async-start(), calls=%async_computation.18 | async-start | bytes 2359296 | tf_op jit(solution)/shard_map/all_gather | solution.py:170
  8.7 151.8 %all-gather.13.cloned.1.call-start = ((), (), s32[]{:S(2)}) async-start(), calls=%async_computation.15 | async-start | bytes 2359296 | tf_op jit(solution)/shard_map/all_gather | solution.py:171
  9.4 253.7 %all-gather.27.cloned.1.call-start = ((), (), s32[]{:S(2)}) async-start(), calls=%async_computation.22 | async-start | bytes 1179648 | tf_op jit(solution)/shard_map/all_gather | solution.py:97
  51.8 382.4 %copy-start.8 = (f32[128,2048]{1,0:T(8,128)}, f32[128,2048]{1,0:T(8,128)S(1)}, u32[]{:S(2)}) copy-start(f32[128,2048]{1,0:T(8,128)S(1)} %reshape.817) | copy-start | bytes 3145732
  147.4 127.0 %all-gather.21.cloned.1.call-start = ((), (), s32[]{:S(2)}) async-start(), calls=%async_computation.19 | async-start | bytes 1179648 | tf_op jit(solution)/shard_map/all_gather | solution.py:97
  148.0 137.7 %all-gather.25.cloned.1.call-start = ((), (), s32[]{:S(2)}) async-start(), calls=%async_computation.21 | async-start | bytes 1179648 | tf_op jit(solution)/shard_map/all_gather | solution.py:98
  163.4 161.7 %all-gather.15.cloned.1.call-start = ((), (), s32[]{:S(2)}) async-start(), calls=%async_computation.16 | async-start | bytes 1179648 | tf_op jit(solution)/shard_map/all_gather | solution.py:98
  166.4 208.9 %all-gather.23.cloned.1.call-start = ((), (), s32[]{:S(2)}) async-start(), calls=%async_computation.20 | async-start | bytes 2359296 | tf_op jit(solution)/shard_map/all_gather | solution.py:172
  167.2 264.8 %all-reduce.22.cloned.1.call-start = ((), (), s32[]{:S(2)}) async-start(), calls=%async_computation.31 | async-start | bytes 4194304 | tf_op jit(solution)/shard_map/psum | solution.py:232
  201.1 236.4 %copy-start.106 = (s32[128,8]{0,1:T(8,128)}, s32[128,8]{0,1:T(8,128)S(1)}, u32[]{:S(2)}) copy-start(s32[128,8]{0,1:T(8,128)S(1)} %copy.327) | copy-start | bytes 12292
  232.9 350.3 %copy-start.52 = (bf16[2048,16]{0,1:T(8,128)(2,1)}, bf16[2048,16]{0,1:T(8,128)(2,1)S(1)}, u32[]{:S(2)}) copy-start(bf16[2048,16]{0,1:T(8,128)(2,1)S(1)} %all_gather.62) | copy-start | bytes 196612
  449.0 120.0 %all-to-all-start.4 = ((bf16[8,2,80,2048]{3,2,1,0:T(8,128)(2,1)}), bf16[8,2,80,2048]{3,2,1,0:T(8,128)(2,1)}, u32[]{:S(2)}, u32[]{:S(2)}) async-start(bf16[8,2,80,2048]{3,2,1,0:T(8,128)(2,1)} %bitcast.448), calls=%async_computation.4 | async-start | bytes 10485760 | tf_op jit(solution)/shard_map/all_to_all | solution.py:291
  569.0 119.2 %all-to-all-start = ((bf16[8,2,80,2048]{3,2,1,0:T(8,128)(2,1)}), bf16[8,2,80,2048]{3,2,1,0:T(8,128)(2,1)}, u32[]{:S(2)}, u32[]{:S(2)}) async-start(bf16[8,2,80,2048]{3,2,1,0:T(8,128)(2,1)} %bitcast.445), calls=%async_computation | async-start | bytes 10485760 | tf_op jit(solution)/shard_map/all_to_all | solution.py:250
  688.2 120.0 %all-to-all-start.6 = ((bf16[8,2,80,2048]{3,2,1,0:T(8,128)(2,1)}), bf16[8,2,80,2048]{3,2,1,0:T(8,128)(2,1)}, u32[]{:S(2)}, u32[]{:S(2)}) async-start(bf16[8,2,80,2048]{3,2,1,0:T(8,128)(2,1)} %bitcast.447), calls=%async_computation.7 | async-start | bytes 10485760 | tf_op jit(solution)/shard_map/all_to_all | solution.py:291
  808.2 120.0 %all-to-all-start.2 = ((bf16[8,2,80,2048]{3,2,1,0:T(8,128)(2,1)}), bf16[8,2,80,2048]{3,2,1,0:T(8,128)(2,1)}, u32[]{:S(2)}, u32[]{:S(2)}) async-start(bf16[8,2,80,2048]{3,2,1,0:T(8,128)(2,1)} %bitcast.446), calls=%async_computation.2 | async-start | bytes 10485760 | tf_op jit(solution)/shard_map/all_to_all | solution.py:250
  828.5 344.8 %copy-start.72 = (bf16[8,2,80,256]{3,2,0,1:T(8,128)(2,1)}, bf16[8,2,80,256]{3,2,0,1:T(8,128)(2,1)S(1)}, u32[]{:S(2)}) copy-start(bf16[8,2,80,256]{3,2,0,1:T(8,128)(2,1)S(1)} %get-tuple-element.73) | copy-start | bytes 1966084
  928.3 119.7 %all-to-all-start.1 = ((bf16[8,2,80,2048]{3,2,1,0:T(8,128)(2,1)}), bf16[8,2,80,2048]{3,2,1,0:T(8,128)(2,1)}, u32[]{:S(2)}, u32[]{:S(2)}) async-start(bf16[8,2,80,2048]{3,2,1,0:T(8,128)(2,1)} %copy.336), calls=%async_computation.1 | async-start | bytes 10485760 | tf_op jit(solution)/shard_map/all_to_all | solution.py:264
  1048.0 119.6 %all-to-all-start.3 = ((bf16[8,2,80,2048]{3,2,1,0:T(8,128)(2,1)}), bf16[8,2,80,2048]{3,2,1,0:T(8,128)(2,1)}, u32[]{:S(2)}, u32[]{:S(2)}) async-start(bf16[8,2,80,2048]{3,2,1,0:T(8,128)(2,1)} %copy.359), calls=%async_computation.3 | async-start | bytes 10485760 | tf_op jit(solution)/shard_map/all_to_all | solution.py:264
  1167.6 231.6 %all-to-all-start.7 = ((f32[8,2,80,2048]{3,2,1,0:T(8,128)}), f32[8,2,80,2048]{3,2,1,0:T(8,128)}, u32[]{:S(2)}, u32[]{:S(2)}) async-start(f32[8,2,80,2048]{3,2,1,0:T(8,128)} %copy.383), calls=%async_computation.8 | async-start | bytes 20971520 | tf_op jit(solution)/shard_map/all_to_all | solution.py:321
  1399.2 232.6 %all-to-all-start.5 = ((f32[8,2,80,2048]{3,2,1,0:T(8,128)}), f32[8,2,80,2048]{3,2,1,0:T(8,128)}, u32[]{:S(2)}, u32[]{:S(2)}) async-start(f32[8,2,80,2048]{3,2,1,0:T(8,128)} %copy.362), calls=%async_computation.5 | async-start | bytes 20971520 | tf_op jit(solution)/shard_map/all_to_all | solution.py:321
  1405.5 300.3 %all-reduce.20.cloned.1.call-start = ((), (), s32[]{:S(2)}) async-start(), calls=%async_computation.30 | async-start | bytes 4194304 | tf_op jit(solution)/shard_map/psum | solution.py:326
  1651.3 141.4 %reduce-scatter.8.cloned.1.call-start = ((), (), s32[]{:S(2)}) async-start(), calls=%async_computation.23 | async-start | bytes 1179648 | tf_op jit(solution)/shard_map/reduce_scatter | solution.py:374
  1730.6 129.0 %reduce-scatter.10.cloned.1.call-start = ((), (), s32[]{:S(2)}) async-start(), calls=%async_computation.24 | async-start | bytes 1179648 | tf_op jit(solution)/shard_map/reduce_scatter | solution.py:374
  1744.3 221.4 %all-reduce.24.cloned.1.call-start = ((), (), s32[]{:S(2)}) async-start(), calls=%async_computation.32 | async-start | bytes 4194304
  1767.5 275.9 %reduce-scatter.20.cloned.1.call-start = ((), (), s32[]{:S(2)}) async-start(), calls=%async_computation.29 | async-start | bytes 73728 | tf_op jit(solution)/shard_map/reduce_scatter | solution.py:447
  1770.0 306.5 %all-reduce.26.cloned.1.call-start = ((), (), s32[]{:S(2)}) async-start(), calls=%async_computation.33 | async-start | bytes 4194304 | tf_op jit(solution)/shard_map/psum | solution.py:269
  1991.3 155.4 %reduce-scatter.18.cloned.1.call-start = ((), (), s32[]{:S(2)}) async-start(), calls=%async_computation.28 | async-start | bytes 2359296 | tf_op jit(solution)/shard_map/reduce_scatter | solution.py:444
  1995.7 221.4 %reduce-scatter.16.cloned.1.call-start = ((), (), s32[]{:S(2)}) async-start(), calls=%async_computation.27 | async-start | bytes 2359296 | tf_op jit(solution)/shard_map/reduce_scatter | solution.py:441
  2001.1 286.7 %reduce-scatter.14.cloned.1.call-start = ((), (), s32[]{:S(2)}) async-start(), calls=%async_computation.26 | async-start | bytes 2359296 | tf_op jit(solution)/shard_map/reduce_scatter | solution.py:438
  2013.2 345.4 %reduce-scatter.12.cloned.1.call-start = ((), (), s32[]{:S(2)}) async-start(), calls=%async_computation.25 | async-start | bytes 2359296 | tf_op jit(solution)/shard_map/reduce_scatter | solution.py:435
  (171 other events, 5287.9 us)
Sparse Core Ops, SparseCore 0:
  10.2 50.2 all-gather.16
  62.6 47.7 all-gather.18
  112.6 47.8 all-gather.12
  162.4 38.8 all-gather.26
  203.3 39.3 all-gather.20
  245.3 38.6 all-gather.24
  286.1 38.9 all-gather.14
  327.2 48.0 all-gather.22
  380.8 51.0 all-reduce.21
  1651.3 54.3 all-reduce.19
  1730.7 61.9 reduce-scatter.7
  1796.9 62.5 reduce-scatter.9
  1863.2 102.5 all-reduce.23
  1968.7 51.4 reduce-scatter.19
  2023.2 53.1 all-reduce.25
  2080.2 66.4 reduce-scatter.17
  2150.5 66.5 reduce-scatter.15
  2220.9 66.8 reduce-scatter.13
  2291.8 66.8 reduce-scatter.11
where the time goes:
time: 2380 us; the launch traced here: 2370 us
  waiting for transfers between devices  1610 us (68%)
  local copies, waits for them, and re-layouts  227 us (10%)
  other arithmetic  163 us (7%)
  blocking collectives  154 us (6%)
  matrix products  151 us (6%)
  starting transfers between devices  46.6 us (2%)
    all_to_all x2, waiting for transfers between devices, shards(): lax.all_to_all(expert_grad, 'ep', split_axis=0, concat_axis=0, tiled=True)  394 us
    all_to_all x2, waiting for transfers between devices, shards(): lax.all_to_all(grad_out.reshape(axis_devices, local_experts, capacity, wi...  210 us
    all_to_all x2, waiting for transfers between devices, shards(): lax.all_to_all(partial_out, 'ep', split_axis=0, concat_axis=0, tiled=True)  200 us
    all_to_all x2, waiting for transfers between devices, shards(): lax.all_to_all(outgoing.reshape(axis_devices, local_experts, capacity, wi...  187 us
    unnamed x20, waiting for transfers between devices  102 us
    reduce_scatter x2, waiting for transfers between devices, shards(): lax.psum_scatter(key_grad_all.astype(jnp.bfloat16), 'ep', scatter_dimensi...  80.1 us
    reduce_scatter x1, waiting for transfers between devices, shards(): lax.psum_scatter(grad_query.astype(jnp.bfloat16), 'ep', scatter_dimension...  69 us
    reduce_scatter x1, waiting for transfers between devices, shards(): lax.psum_scatter(grad_key.astype(jnp.bfloat16), 'ep', scatter_dimension=0...  68.9 us
  transfers between devices with their start and end apart: 27, of which 23 were waited for; matrix products, arithmetic and copies ran while one was open for 20% of the time, Pallas kernels for 0%

commit v1 on v0

--- a/solution.py
+++ b/solution.py
@@ -1,6 +1,9 @@
 import jax
 import jax.numpy as jnp
+import numpy as np
 from jax import lax
+from jax.experimental import pallas as pl
+from jax.experimental.pallas import tpu as pltpu
 from jax.sharding import PartitionSpec as P
 
 HEAD_DIM = 128
@@ -111,7 +114,7 @@
     )
 
 
-def shards(
+def routed_shards(
     inputs,
     lengths,
     routes,
@@ -239,8 +242,14 @@
         picked = named_rows[:, :, None] == expert_numbers[None, None, :]
         picked_float = picked.astype(jnp.float32)
         gates = jnp.sum(picked_float * probs[:, None, :], axis=-1)
-        flat_pick = picked.reshape(row_count * top_count, expert_count).astype(jnp.int32)
-        places = jnp.sum((jnp.cumsum(flat_pick, axis=0) - 1) * flat_pick, axis=1)
+        chosen_rows = jnp.sum(picked_float, axis=1)
+        before = jnp.arange(row_count)[:, None] > jnp.arange(row_count)[None, :]
+        earlier = jnp.dot(
+            before.astype(jnp.bfloat16),
+            chosen_rows.astype(jnp.bfloat16),
+            preferred_element_type=jnp.float32,
+        )
+        places = jnp.sum(picked_float * earlier[:, None, :], axis=-1).astype(jnp.int32).reshape(-1)
         slots = named_rows.reshape(-1) * capacity + places
         outgoing = (
             jnp.zeros((expert_count * capacity, width), jnp.bfloat16)
@@ -476,6 +485,1570 @@
         grad_up,
         grad_down,
     )
+
+
+MESH = pl.DeviceIdType.MESH
+ANYWHERE = pl.BlockSpec(memory_space=pl.ANY)
+IN_VMEM = pl.BlockSpec(memory_space=pltpu.VMEM)
+LANES = 128
+BLOCK_BITS = ("y", "x", "z", "c")
+HEAD_BITS = ("x", "z", "c", "y")
+TURNS = (("z", "x", "y"), ("x", "y", "z"), ("y", "z", "x"))
+
+
+def place_bits():
+    ep = lax.axis_index("ep")
+    tp = lax.axis_index("tp")
+    return {
+        "h": ep // 4,
+        "z": (ep // 2) % 2,
+        "x": ep % 2,
+        "y": tp // 2,
+        "c": tp % 2,
+    }
+
+
+def device_of(bits):
+    return {"ep": 4 * bits["h"] + 2 * bits["z"] + bits["x"], "tp": 2 * bits["y"] + bits["c"]}
+
+
+def flipped(bits, *names):
+    turned = dict(bits)
+    for name in names:
+        turned[name] = 1 - turned[name]
+    return device_of(turned)
+
+
+def block_index(bits, order):
+    return sum(bits[name] * (1 << k) for k, name in enumerate(order))
+
+
+def held_segments(bits, gathered, order):
+    run = 0
+    while run < len(order) and order[run] in gathered:
+        run += 1
+    base, combos = 0, [0]
+    for k in range(run, len(order)):
+        weight = LANES << k
+        if order[k] in gathered:
+            combos = [v + s * weight for v in combos for s in (0, 1)]
+        else:
+            base = base + bits[order[k]] * weight
+    return [(pl.multiple_of(base + v, LANES), LANES << run) for v in combos]
+
+
+class Wires:
+    def __init__(self, bits, send, recv):
+        self.bits, self.send, self.recv = bits, send, recv
+        self.count, self.pending = 0, []
+
+    def start(self, source, target, *names):
+        k = self.count
+        self.count += 1
+        copy = pltpu.make_async_remote_copy(
+            src_ref=source,
+            dst_ref=target,
+            send_sem=self.send.at[k],
+            recv_sem=self.recv.at[k],
+            device_id=flipped(self.bits, *names),
+            device_id_type=MESH,
+        )
+        copy.start()
+        self.pending.append(copy)
+        return copy
+
+    def settle(self, copy):
+        copy.wait()
+        self.pending = [other for other in self.pending if other is not copy]
+
+    def sent(self, copies):
+        for copy in copies:
+            copy.wait_send()
+        self.pending = [other for other in self.pending if all(other is not c for c in copies)]
+
+    def finish(self):
+        for copy in self.pending:
+            copy.wait_send()
+
+
+def greet(bits, partners):
+    barrier = pltpu.get_barrier_semaphore()
+    for names in partners:
+        pl.semaphore_signal(
+            barrier, inc=1, device_id=flipped(bits, *names), device_id_type=MESH
+        )
+    pl.semaphore_wait(barrier, len(partners))
+
+
+def receive(copies):
+    for copy in copies:
+        copy.wait_recv()
+
+
+EP_MASKS = (("z",), ("x",), ("z", "x"), ("h",), ("h", "z"), ("h", "x"), ("h", "z", "x"))
+
+
+CUBE_MASKS = tuple(
+    tuple(n for k, n in enumerate("zxyc") if mask >> k & 1) for mask in range(1, 16)
+)
+
+
+ALL_MASKS = CUBE_MASKS + (("h",),) + tuple(("h",) + names for names in CUBE_MASKS)
+
+
+def semaphores(count):
+    return [pltpu.SemaphoreType.DMA((count,)), pltpu.SemaphoreType.DMA((count,))]
+
+
+def spread_kernel(
+    inp, wq, wk, wv, small,
+    xg, wh, sm,
+    local, send, recv,
+):
+    bits = place_bits()
+    h, z, x, y, c = (bits[n] for n in "hzxyc")
+    wires = Wires(bits, send, recv)
+    locals_ = []
+
+    def keep(source, target):
+        copy = pltpu.make_async_copy(source, target, local.at[len(locals_)])
+        copy.start()
+        locals_.append(copy)
+
+    cuts = ((0, 384), (384, 384), (768, 256), (1024, 384), (1408, 384), (1792, 256))
+    x_first = [
+        wires.start(
+            inp.at[1 - h, y, c, :, pl.ds(lo, n)], xg.at[y, h, z, x, c, :, pl.ds(lo, n)], "h"
+        )
+        for lo, n in cuts
+    ]
+    keep(inp.at[h, y, c], xg.at[y, h, z, x, c])
+    small_copies = [wires.start(small, sm.at[h, z, x], *names) for names in EP_MASKS]
+    keep(small, sm.at[h, z, x])
+    head_copies = []
+    for m, weight in enumerate((wq, wk, wv)):
+        for names in EP_MASKS:
+            if "h" not in names:
+                continue
+            tz = 1 - z if "z" in names else z
+            tx = 1 - x if "x" in names else x
+            cols = pl.ds(pl.multiple_of((2 * tz + tx) * LANES, LANES), LANES)
+            head_copies.append(
+                wires.start(
+                    weight.at[:, cols], wh.at[h, z, x, :, pl.ds(m * LANES, LANES)], *names
+                )
+            )
+    for m, weight in enumerate((wq, wk, wv)):
+        for names in EP_MASKS:
+            if "h" in names:
+                continue
+            tz = 1 - z if "z" in names else z
+            tx = 1 - x if "x" in names else x
+            cols = pl.ds(pl.multiple_of((2 * tz + tx) * LANES, LANES), LANES)
+            head_copies.append(
+                wires.start(
+                    weight.at[:, cols], wh.at[h, z, x, :, pl.ds(m * LANES, LANES)], *names
+                )
+            )
+        own = pl.ds(pl.multiple_of((2 * z + x) * LANES, LANES), LANES)
+        keep(weight.at[:, own], wh.at[h, z, x, :, pl.ds(m * LANES, LANES)])
+    for copy in locals_:
+        copy.wait()
+
+    def slot(ref, gathered, lo, n):
+        pick = tuple(
+            slice(None) if name == "h" or name in gathered else bits[name] for name in "yhzxc"
+        )
+        return ref.at[pick + (slice(None), pl.ds(lo, n))]
+
+    for ref, first in ((xg, x_first),):
+        arriving = [[copy] for copy in first]
+        gathered = [set() for _ in cuts]
+        for stage in range(4):
+            for k, (lo, n) in enumerate(cuts):
+                receive(arriving[k])
+                name = (TURNS[k % 3] + ("c",))[stage]
+                part = slot(ref, gathered[k], lo, n)
+                arriving[k] = [wires.start(part, part, name)]
+                gathered[k] = gathered[k] | {name}
+        for copies in arriving:
+            receive(copies)
+    receive(head_copies)
+    receive(small_copies)
+    wires.finish()
+
+
+def spread_inputs(inp, wq, wk, wv, small):
+    micro, rows, width = inp.shape
+    cut = (micro, 2, 2, rows // 4, width)
+    xg, wh, sm = pl.pallas_call(
+        spread_kernel,
+        out_shape=(
+            jax.ShapeDtypeStruct((2, 2, 2, 2, 2, rows // 4, width), jnp.bfloat16),
+            jax.ShapeDtypeStruct((2, 2, 2, wq.shape[0], 3 * LANES), jnp.bfloat16),
+            jax.ShapeDtypeStruct((2, 2, 2) + small.shape, small.dtype),
+        ),
+        in_specs=[ANYWHERE] * 5,
+        out_specs=[ANYWHERE] * 3,
+        scratch_shapes=[pltpu.SemaphoreType.DMA((16,)), *semaphores(96)],
+        compiler_params=pltpu.CompilerParams(has_side_effects=True),
+    )(inp.reshape(cut), wq, wk, wv, small)
+    return (
+        xg.reshape(8 * rows, width),
+        wh.reshape(width, 3 * LANES),
+        sm.reshape(8, *small.shape),
+    )
+
+
+def row_cuts(rows):
+    step = -(-rows // 96) * 16
+    return [
+        (lo, min(step, rows - lo), TURNS[k % 3] + ("c",))
+        for k, lo in enumerate(range(0, rows, step))
+    ]
+
+
+def start_stage(wires, bits, order, block, whole, lead, lo, n, gathered, name):
+    copies = []
+    for offset, width in held_segments(bits, gathered, order):
+        target = whole.at[lead + (pl.ds(lo, n), pl.ds(offset, width))]
+        source = target if gathered else block.at[pl.ds(lo, n)]
+        copies.append(wires.start(source, target, name))
+    return copies
+
+
+def add_strips(target, left, right):
+    rows = target.shape[0]
+    step = 32
+
+    def strip(k, carry):
+        at = pl.ds(pl.multiple_of(k * step, step), step)
+        total = left[at].astype(jnp.float32) + right[at].astype(jnp.float32)
+        target[at] = total.astype(target.dtype)
+        return carry
+
+    lax.fori_loop(0, rows // step, strip, 0)
+
+
+class Reduction:
+    def __init__(self, wires, bits, source, turns, buffers, local):
+        self.wires, self.bits, self.source = wires, bits, source
+        self.turns, self.buffers, self.local = turns, buffers, local
+        self.order = ["y", "x", "z"]
+
+    def start(self):
+        b = self.buffers
+        half = 8 * LANES
+        c = self.bits["c"]
+        mine = pl.ds(pl.multiple_of(c * half, half), half)
+        other = pl.ds(pl.multiple_of((1 - c) * half, half), half)
+        self.copies = [self.wires.start(self.source.at[:, other], b["r"][0], "c")]
+        self.loaded = pltpu.make_async_copy(self.source.at[:, mine], b["a"][0], self.local)
+        self.loaded.start()
+
+    def pieces(self, name):
+        k = self.order.index(name)
+        count = len(self.order)
+        width = LANES << k
+        kept, sent = [], []
+        for s in range(1 << (count - 1 - k)):
+            base = s * 2 * width
+            near = pl.multiple_of(base + self.bits[name] * width, LANES)
+            far = pl.multiple_of(base + (1 - self.bits[name]) * width, LANES)
+            kept.append((near, s * width, width))
+            sent.append((far, s * width, width))
+        return kept, sent
+
+    def step(self, stage):
+        b = self.buffers
+        receive(self.copies)
+        if stage == 1:
+            self.loaded.wait()
+            add_strips(b["a"][0], b["a"][0], b["r"][0])
+        else:
+            name = self.turns[stage - 2]
+            kept, _ = self.pieces(name)
+            for at, to, width in kept:
+                add_strips(
+                    b["a"][stage - 1].at[:, pl.ds(to, width)],
+                    b["a"][stage - 2].at[:, pl.ds(at, width)],
+                    b["r"][stage - 1].at[:, pl.ds(to, width)],
+                )
+            self.order = [n for n in self.order if n != name]
+        if stage == 4:
+            return
+        name = self.turns[stage - 1]
+        _, sent = self.pieces(name)
+        self.copies = [
+            self.wires.start(
+                b["a"][stage - 1].at[:, pl.ds(at, width)],
+                b["r"][stage].at[:, pl.ds(to, width)],
+                name,
+            )
+            for at, to, width in sent
+        ]
+
+
+def reduction_buffers(count, rows):
+    widths = [8 * LANES, 4 * LANES, 2 * LANES, LANES]
+    shapes = []
+    for width in widths:
+        shapes.append(pltpu.VMEM((count, rows, width), jnp.bfloat16))
+        shapes.append(pltpu.VMEM((count, rows, width), jnp.bfloat16))
+    return shapes
+
+
+def buffers_of(scratch, k):
+    return {
+        "a": [scratch[2 * s].at[k] for s in range(4)],
+        "r": [scratch[2 * s + 1].at[k] for s in range(4)],
+    }
+
+
+STRIP = 256
+
+
+def reductions(wires, bits, pool, local, sources):
+    chunks = []
+    for k, (source, what) in enumerate(sources):
+        chunk = Reduction(wires, bits, source, TURNS[k % 3], buffers_of(pool, k), local.at[k])
+        chunk.what = what
+        chunks.append(chunk)
+    for chunk in chunks:
+        chunk.start()
+    return chunks
+
+
+EXPERT_ROWS = 512
+STRIP_ROWS = 32
+BLOCK_CUTS = ((0, 192, TURNS[0]), (192, 160, TURNS[1]), (352, 160, TURNS[2]))
+
+
+def rows_dot(left, right):
+    return lax.dot_general(
+        left, right, (((0,), (0,)), ((), ())), preferred_element_type=jnp.float32
+    )
+
+
+def half_pieces(bits, order, name):
+    k = order.index(name)
+    width = LANES << k
+    kept, sent = [], []
+    for s in range(1 << (len(order) - 1 - k)):
+        base = s * 2 * width
+        near = pl.multiple_of(base + bits[name] * width, LANES)
+        far = pl.multiple_of(base + (1 - bits[name]) * width, LANES)
+        kept.append((near, s * width, width))
+        sent.append((far, s * width, width))
+    return kept, sent
+
+
+def add_into(target, source, step=32):
+    def strip(k, carry):
+        at = pl.ds(pl.multiple_of(k * step, step), step)
+        total = target[at].astype(jnp.float32) + source[at].astype(jnp.float32)
+        target[at] = total.astype(target.dtype)
+        return carry
+
+    lax.fori_loop(0, target.shape[0] // step, strip, 0)
+
+
+def experts_kernel(
+    attended, wo, x_block, gain, grads_all, w_gate_in, w_up_in, w_down_in, router_in, mask_in,
+    middle, gained, wh, out_part, normed_total, tiny_out, logits_own, gate_out, up_out, down_out,
+    w_gate, w_up, w_down, router, mask, grad_gate, grad_up, grad_down,
+    wor, squares, rows_all, grads, out, normed, inner_low, left_low, all_squares,
+    a_full, b_full, du_full, gates_full, scale_full, terms,
+    r0, r1, r2, r3, cross, tiny_sum, tiny_in,
+    local, load, store, read, write, gather_send, gather_recv, scatter_send, scatter_recv,
+    cross_send, cross_recv, tiny_sems, wo_send, wo_recv, send, recv,
+):
+    bits = place_bits()
+    h, z, x, y, c = (bits[n] for n in "hzxyc")
+    ep = 4 * h + 2 * z + x
+    local_experts = w_gate.shape[0]
+    width, hidden = rows_all.shape[2], w_gate.shape[2]
+    expert_count = 8 * local_experts
+    wires = Wires(bits, send, recv)
+    [(offset, _)] = held_segments(bits, (), BLOCK_BITS)
+    own_cols = pl.ds(offset, LANES)
+    blocks = 4
+    tile = width // 4
+
+    def is_foreign(k):
+        return ((k + 1) // 2) % 2
+
+    def micro_of(k):
+        return h + is_foreign(k) * (1 - 2 * h)
+
+    def start_of(k):
+        return pl.multiple_of((k // 2) * EXPERT_ROWS, EXPERT_ROWS)
+
+    def remote(source, target, s_sem, r_sem, *names):
+        return pltpu.make_async_remote_copy(
+            src_ref=source,
+            dst_ref=target,
+            send_sem=s_sem,
+            recv_sem=r_sem,
+            device_id=flipped(bits, *names),
+            device_id_type=MESH,
+        )
+
+    def gather_copies(k, stage):
+        copies, index = [], 0
+        for lo, n, turns in BLOCK_CUTS:
+            order = turns + ("c",)
+            for s in range(4):
+                for seg, wide in held_segments(bits, order[:s], BLOCK_BITS):
+                    if s == stage:
+                        part = rows_all.at[
+                            micro_of(k), pl.ds(start_of(k) + lo, n), pl.ds(seg, wide)
+                        ]
+                        copies.append(
+                            remote(
+                                part, part, gather_send.at[k, index], gather_recv.at[k, index], order[s]
+                            )
+                        )
+                    index += 1
+        return copies
+
+    def gather_step(k, stage):
+        if stage > 0:
+            for copy in gather_copies(k, stage - 1):
+                copy.wait_recv()
+        if stage < 4:
+            for copy in gather_copies(k, stage):
+                copy.start()
+        else:
+            for s in range(4):
+                for copy in gather_copies(k, s):
+                    copy.wait_send()
+
+    held = (r0, r1, r2, r3)
+
+    def scatter_copies(k, stage):
+        copies, index = [], 0
+        for a, source in enumerate((normed,)):
+            for lo, n, turns in BLOCK_CUTS:
+                order = ["y", "x", "z"]
+                at = pl.ds(lo, n)
+                for s in range(4):
+                    if s == 0:
+                        other = pl.ds(pl.multiple_of((1 - c) * 8 * LANES, 8 * LANES), 8 * LANES)
+                        pairs = [(source.at[at, other], r0.at[k, a, at])]
+                        name = "c"
+                    else:
+                        name = turns[s - 1]
+                        _, sent = half_pieces(bits, order, name)
+                        pairs = [
+                            (
+                                held[s - 1].at[k, a, at, pl.ds(far, wide)],
+                                held[s].at[k, a, at, pl.ds(to, wide)],
+                            )
+                            for far, to, wide in sent
+                        ]
+                        order = [n_ for n_ in order if n_ != name]
+                    for src, dst in pairs:
+                        if s == stage:
+                            copies.append(
+                                remote(
+                                    src, dst, scatter_send.at[k, index], scatter_recv.at[k, index], name
+                                )
+                            )
+                        index += 1
+        return copies
+
+    def scatter_add(k, stage):
+        for a, source in enumerate((normed,)):
+            if stage == 0:
+                mine = pl.ds(pl.multiple_of(c * 8 * LANES, 8 * LANES), 8 * LANES)
+                add_into(r0.at[k, a], source.at[:, mine])
+                continue
+            for lo, n, turns in BLOCK_CUTS:
+                order = [b for b in ("y", "x", "z") if b not in turns[: stage - 1]]
+                kept, _ = half_pieces(bits, order, turns[stage - 1])
+                at = pl.ds(lo, n)
+                for near, to, wide in kept:
+                    add_into(
+                        held[stage].at[k, a, at, pl.ds(to, wide)],
+                        held[stage - 1].at[k, a, at, pl.ds(near, wide)],
+                    )
+
+    def cross_copies(k):
+        half = k // 2
+        return [
+            remote(
+                r3.at[k, a],
+                cross.at[a, pl.ds(start_of(k), EXPERT_ROWS)],
+                cross_send.at[a, half],
+                cross_recv.at[a, half],
+                "h",
+            )
+            for a in range(1)
+        ]
+
+    def scatter_step(k, stage):
+        if stage > 0:
+            for copy in scatter_copies(k, stage - 1):
+                copy.wait()
+            scatter_add(k, stage - 1)
+        if stage < 4:
+            for copy in scatter_copies(k, stage):
+                copy.start()
+        else:
+
+            @pl.when(is_foreign(k) == 1)
+            def _():
+                for copy in cross_copies(k):
+                    copy.start()
+
+    def grad_read(k):
+        s = k % 2
+        return pltpu.make_async_copy(
+            grads_all.at[:, micro_of(k), k // 2],
+            grads.at[s].reshape(grads_all.shape[0], grads_all.shape[3], width),
+            read.at[s],
+        )
+
+    def tiny_copy(stage):
+        return remote(
+            tiny_sum, tiny_in.at[stage], tiny_sems.at[0, stage], tiny_sems.at[1, stage], "cy"[stage]
+        )
+
+    def out_write(k):
+        return pltpu.make_async_copy(
+            out, out_part.at[micro_of(k), pl.ds(start_of(k), EXPERT_ROWS)], write
+        )
+
+    tp = 2 * y + c
+    halves = (out, normed)
+    [(head_offset, _)] = held_segments(bits, (), HEAD_BITS)
+    own = []
+    for half in (0, 1):
+        at = pl.ds(half * EXPERT_ROWS, EXPERT_ROWS)
+        own.append(
+            pltpu.make_async_copy(
+                attended.at[at], halves[half].at[:, pl.ds(head_offset, LANES)], local.at[3 * half]
+            )
+        )
+        own[half].start()
+    grad_read(0).start()
+    loads = [
+        pltpu.make_async_copy(source, target, load.at[n])
+        for n, (source, target) in enumerate(
+            (
+                (router_in, router),
+                (mask_in, mask),
+                (w_gate_in, w_gate),
+                (w_up_in, w_up),
+                (w_down_in, w_down),
+            )
+        )
+    ]
+    for copy in loads:
+        copy.start()
+    greet(bits, ALL_MASKS)
+    arriving = [[[] for _ in BLOCK_CUTS] for _ in halves]
+    heads_sent = []
+
+    def heads_stage(half, stage):
+        for n, (lo, count, turns) in enumerate(BLOCK_CUTS):
+            order = turns + ("c",)
+            receive(arriving[half][n])
+            arriving[half][n] = []
+            if stage == 4:
+                continue
+            for seg, wide in held_segments(bits, order[:stage], HEAD_BITS):
+                part = halves[half].at[pl.ds(lo, count), pl.ds(seg, wide)]
+                arriving[half][n].append(wires.start(part, part, order[stage]))
+            heads_sent.extend(arriving[half][n])
+
+    for half in (0, 1):
+        own[half].wait()
+        heads_stage(half, 0)
+    def output_row_copy(a, p):
+        ty = 1 - y if p else y
+        rows = pl.ds(pl.multiple_of(ty * LANES, LANES), LANES)
+        cols = pl.ds(pl.multiple_of(tp * 4 * LANES, LANES), 4 * LANES)
+        return pltpu.make_async_remote_copy(
+            src_ref=wo.at[rows],
+            dst_ref=wor.at[:, cols],
+            send_sem=wo_send.at[2 * a + p],
+            recv_sem=wo_recv.at[tp],
+            device_id=device_of({"h": 1 - h if a else h, "z": z, "x": x, "y": ty, "c": h}),
+            device_id_type=MESH,
+        )
+
+    def own_row_copy():
+        rows = pl.ds(pl.multiple_of(y * LANES, LANES), LANES)
+        cols = pl.ds(pl.multiple_of(tp * 4 * LANES, LANES), 4 * LANES)
+        return pltpu.make_async_copy(wo.at[rows], wor.at[:, cols], local.at[1])
+
+    for a in (0, 1):
+        for p in (0, 1):
+            if a == 0 and p == 0:
+                pl.when(c != h)(lambda: output_row_copy(0, 0).start())
+                pl.when(c == h)(lambda: own_row_copy().start())
+            else:
+                output_row_copy(a, p).start()
+    def head_columns(tz, tx):
+        return wo.at[:, pl.ds(pl.multiple_of((2 * tz + tx) * LANES, LANES), LANES)]
+
+    head_copies = [
+        wires.start(
+            head_columns(1 - z if "z" in names else z, 1 - x if "x" in names else x),
+            wh.at[h, z, x],
+            *names,
+        )
+        for names in EP_MASKS
+    ]
+    own_head = pltpu.make_async_copy(head_columns(z, x), wh.at[h, z, x], local.at[2])
+    own_head.start()
+    for stage in (1, 2, 3):
+        for half in (0, 1):
+            heads_stage(half, stage)
+    for source in range(4):
+        sy, sc = source // 2, source % 2
+
+        def arrived(source=source):
+            pltpu.make_async_remote_copy(
+                src_ref=wo.at[pl.ds(0, LANES)],
+                dst_ref=wor.at[:, pl.ds(source * 4 * LANES, 4 * LANES)],
+                send_sem=wo_send.at[0],
+                recv_sem=wo_recv.at[source],
+                device_id=flipped(bits, "h"),
+                device_id_type=MESH,
+            ).wait_recv()
+
+        pl.when(jnp.logical_or(c != h, tp != source))(arrived)
+    pl.when(c == h)(lambda: own_row_copy().wait())
+    for a in (0, 1):
+        for p in (0, 1):
+            if a == 0 and p == 0:
+                pl.when(c != h)(lambda: output_row_copy(0, 0).wait_send())
+            else:
+                output_row_copy(a, p).wait_send()
+    crossing, square_copies = [], []
+
+    def project(half):
+        heads_stage(half, 4)
+        at = pl.ds(half * EXPERT_ROWS, EXPERT_ROWS)
+        rows_now = x_block[at].astype(jnp.float32) + contract_cols(halves[half][...], wor[...])
+        middle[at] = rows_now
+        low = (rows_now * gain[0:1]).astype(jnp.bfloat16)
+        gained[at] = low
+        rows_all[h, at, own_cols] = low
+        lines = row_lines(rows_now * rows_now)
+        squares[half] = jnp.concatenate([lines, lines], axis=0)
+        all_squares[half, h, c, z, x, y] = squares[half]
+
+    def announce(half):
+        at = pl.ds(half * EXPERT_ROWS, EXPERT_ROWS)
+        part = rows_all.at[h, at, own_cols]
+        square_copies.append(
+            [
+                wires.start(squares.at[half], all_squares.at[half, h, c, z, x, y], *names)
+                for names in CUBE_MASKS
+            ]
+        )
+        crossing.append(wires.start(part, part, "h"))
+
+    project(0)
+    gather_step(0, 0)
+    announce(0)
+    project(1)
+    gather_step(0, 1)
+    announce(1)
+    gather_step(0, 2)
+    for copies in square_copies:
+        receive(copies)
+    square_cross = wires.start(all_squares.at[:, h], all_squares.at[:, h], "h")
+    gather_step(0, 3)
+    crossing[0].wait_recv()
+    gather_step(1, 0)
+    gather_step(0, 4)
+    gather_step(1, 1)
+    receive(head_copies)
+    own_head.wait()
+    wires.sent(heads_sent)
+    grad_gate[...] = jnp.zeros_like(grad_gate)
+    grad_up[...] = jnp.zeros_like(grad_up)
+    grad_down[...] = jnp.zeros_like(grad_down)
+    for copy in loads:
+        copy.wait()
+
+    @pl.loop(0, blocks)
+    def _(k):
+        slot = k % 2
+        micro, first = micro_of(k), start_of(k)
+        at = pl.ds(first, EXPERT_ROWS)
+        rows = rows_all.at[micro, at]
+        grad = grads.at[slot]
+        more, two_more, before = k < blocks - 1, k < blocks - 2, k > 0
+        last = k == blocks - 1
+
+        def when(flag, step, which, stage):
+            pl.when(flag)(lambda: step(which, stage))
+
+        pl.when(more)(lambda: grad_read(k + 1).start())
+        pl.when(k == 1)(square_cross.wait_recv)
+        when(more, gather_step, k + 1, 2)
+        grad_read(k).wait()
+
+        sums = jnp.sum(all_squares[k // 2, micro].reshape(16, 8, LANES), axis=0)
+        scales = lax.rsqrt(sums / width + EPSILON)
+        for s in range(4):
+            scale_full[pl.ds(s * LANES, LANES)] = jnp.broadcast_to(
+                scales[s : s + 1], (LANES, LANES)
+            ).T
+        logits = scale_full[...] * jnp.dot(
+            rows[...], router[...], preferred_element_type=jnp.float32
+        )
+        lane = lax.broadcasted_iota(jnp.int32, logits.shape, 1)
+
+        @pl.when(is_foreign(k) == 0)
+        def _():
+            logits_own[at] = jnp.where(lane == expert_count, scale_full[...], logits)
+
+        shown = jnp.where(lane < expert_count, logits, NEGATIVE)
+        weights = jnp.exp(shown - jnp.max(shown, axis=1, keepdims=True))
+        gates = weights / jnp.sum(weights, axis=1, keepdims=True)
+        gates = gates * mask[micro, at].astype(jnp.float32)
+        for e in range(local_experts):
+            gate = jnp.sum(
+                jnp.where(lane == ep * local_experts + e, gates, 0.0), axis=1, keepdims=True
+            )
+            gates_full[e] = jnp.broadcast_to(gate, logits.shape)
+        for e in range(local_experts):
+            a_full[...] = jnp.dot(rows[...], w_gate[e], preferred_element_type=jnp.float32)
+            b_full[...] = jnp.dot(rows[...], w_up[e], preferred_element_type=jnp.float32)
+            du_full[...] = contract_cols(grad[...], w_down[e])
+
+            @pl.loop(0, EXPERT_ROWS // STRIP_ROWS, unroll=2)
+            def _(n):
+                part = pl.ds(pl.multiple_of(n * STRIP_ROWS, STRIP_ROWS), STRIP_ROWS)
+                scale, gate = scale_full[part], gates_full[e, part]
+                for lo in range(0, hidden, LANES):
+                    cols = pl.ds(lo, LANES)
+                    a = scale * a_full[part, cols]
+                    b = scale * b_full[part, cols]
+                    du = du_full[part, cols]
+                    sigma = 0.5 * jnp.tanh(0.5 * a) + 0.5
+                    active = a * sigma
+                    u = active * b
+                    inner_low[e, part, cols] = (u * gate).astype(jnp.bfloat16)
+                    terms[part, pl.ds(e * hidden + lo, LANES)] = (u * du).astype(jnp.bfloat16)
+                    du = du * gate
+                    da = du * b * (sigma + active * (1.0 - sigma))
+                    db = du * active
+                    terms[part, pl.ds((local_experts + e) * hidden + lo, LANES)] = (
+                        da * a + db * b
+                    ).astype(jnp.bfloat16)
+                    left_low[2 * e, part, cols] = (da * scale).astype(jnp.bfloat16)
+                    left_low[2 * e + 1, part, cols] = (db * scale).astype(jnp.bfloat16)
+
+            if e == 0:
+                when(before, scatter_step, k - 1, 2)
+                when(more, gather_step, k + 1, 3)
+        shape = (8, 2 * local_experts * hidden)
+        line = lax.broadcasted_iota(jnp.int32, shape, 0)
+        owner = jnp.minimum(lax.broadcasted_iota(jnp.int32, shape, 1) // hidden, local_experts)
+        tiny_sum[micro, :, at] = contract_cols((line == owner).astype(jnp.bfloat16), terms[...])
+        pl.when(last)(lambda: tiny_copy(0).start())
+        when(before, scatter_step, k - 1, 3)
+
+        @pl.loop(0, 4)
+        def _(t):
+            cols = pl.ds(pl.multiple_of(t * tile, tile), tile)
+            total = jnp.zeros((EXPERT_ROWS, tile), jnp.float32)
+            for e in range(local_experts):
+                total += contract_cols(left_low[2 * e], w_gate[e, cols])
+                total += contract_cols(left_low[2 * e + 1], w_up[e, cols])
+            normed[:, cols] = total.astype(jnp.bfloat16)
+
+        scatter_step(k, 0)
+
+        @pl.when(k == 0)
+        def _():
+            crossing[1].wait_recv()
+
+        when(two_more, gather_step, k + 2, 0)
+        pl.when(before)(lambda: out_write(k - 1).wait())
+
+        @pl.loop(0, 4)
+        def _(t):
+            cols = pl.ds(pl.multiple_of(t * tile, tile), tile)
+            total = jnp.dot(inner_low[0], w_down[0, :, cols], preferred_element_type=jnp.float32)
+            for e in range(1, local_experts):
+                total += jnp.dot(
+                    inner_low[e], w_down[e, :, cols], preferred_element_type=jnp.float32
+                )
+            out[:, cols] = total.astype(jnp.bfloat16)
+
+        when(before, scatter_step, k - 1, 4)
+
+        @pl.when(is_foreign(k) == 0)
+        def _():
+            total = out[:, own_cols].astype(jnp.float32) + middle[at]
+            out[:, own_cols] = total.astype(jnp.bfloat16)
+
+        out_write(k).start()
+
+        @pl.when(last)
+        def _():
+            tiny_copy(0).wait()
+            tiny_sum[...] += tiny_in[0]
+            tiny_copy(1).start()
+
+        def add_grads(lo, hi):
+            @pl.loop(lo, hi)
+            def _(t):
+                cols = pl.ds(pl.multiple_of(t * tile, tile), tile)
+                part = rows[:, cols]
+                grad_part = grad[:, cols]
+                for e in range(local_experts):
+                    grad_gate[e, cols] += rows_dot(part, left_low[2 * e])
+                    grad_up[e, cols] += rows_dot(part, left_low[2 * e + 1])
+                    grad_down[e, :, cols] += rows_dot(inner_low[e], grad_part)
+
+        add_grads(0, 2)
+        scatter_step(k, 1)
+        when(more, gather_step, k + 1, 4)
+        when(two_more, gather_step, k + 2, 1)
+        add_grads(2, 4)
+
+    stores = [
+        pltpu.make_async_copy(source, target, store.at[n])
+        for n, (source, target) in enumerate(
+            ((grad_gate, gate_out), (grad_up, up_out), (grad_down, down_out))
+        )
+    ]
+    for copy in stores:
+        copy.start()
+    tiny_copy(1).wait()
+    tiny_sum[...] += tiny_in[1]
+    slot = tiny_out.at[h, z, x]
+    slot[...] = tiny_sum[h]
+    tiny_copies = [
+        wires.start(tiny_sum.at[1 - h if "h" in names else h], slot, *names)
+        for names in EP_MASKS
+    ]
+    scatter_step(blocks - 1, 2)
+    scatter_step(blocks - 1, 3)
+    scatter_step(blocks - 1, 4)
+    for k in (1, 2):
+        for copy in cross_copies(k):
+            copy.wait()
+    for half, k in ((0, 0), (1, 3)):
+        at = pl.ds(half * EXPERT_ROWS, EXPERT_ROWS)
+        normed_total[at] = r3[k, 0].astype(jnp.float32) + cross[0, at].astype(jnp.float32)
+    out_write(blocks - 1).wait()
+    for copy in stores:
+        copy.wait()
+    receive(tiny_copies)
+    wires.finish()
+
+
+def run_experts(
+    attended, wo, x_block, gain, grads_all, w_gate, w_up, w_down, router, mask, collective_id
+):
+    f32, bf16 = jnp.float32, jnp.bfloat16
+    rows = attended.shape[0]
+    width = grads_all.shape[-1]
+    hidden = w_gate.shape[2]
+    local_experts = w_gate.shape[0]
+    part = (EXPERT_ROWS, width)
+    return pl.pallas_call(
+        experts_kernel,
+        out_shape=(
+            jax.ShapeDtypeStruct((rows, LANES), f32),
+            jax.ShapeDtypeStruct((rows, LANES), bf16),
+            jax.ShapeDtypeStruct((2, 2, 2, wo.shape[0], LANES), bf16),
+            jax.ShapeDtypeStruct((2, rows, width), bf16),
+            jax.ShapeDtypeStruct((rows, LANES), f32),
+            jax.ShapeDtypeStruct((2, 2, 2, 8, rows), f32),
+            jax.ShapeDtypeStruct((rows, LANES), f32),
+            jax.ShapeDtypeStruct(w_gate.shape, f32),
+            jax.ShapeDtypeStruct(w_up.shape, f32),
+            jax.ShapeDtypeStruct(w_down.shape, f32),
+        ),
+        in_specs=[ANYWHERE] * 2 + [IN_VMEM] * 2 + [ANYWHERE] * 6,
+        out_specs=[IN_VMEM] * 2 + [ANYWHERE] * 2 + [IN_VMEM] * 3 + [ANYWHERE] * 3,
+        scratch_shapes=[
+            *[pltpu.VMEM(w.shape, bf16) for w in (w_gate, w_up, w_down)],
+            pltpu.VMEM(router.shape, bf16),
+            pltpu.VMEM(mask.shape, bf16),
+            *[pltpu.VMEM(w.shape, f32) for w in (w_gate, w_up, w_down)],
+            pltpu.VMEM((LANES, width), bf16),
+            pltpu.VMEM((2, 8, LANES), f32),
+            pltpu.VMEM((2, rows, width), bf16),
+            pltpu.VMEM((2,) + part, bf16),
+            pltpu.VMEM(part, bf16),
+            pltpu.VMEM(part, bf16),
+            pltpu.VMEM((local_experts, EXPERT_ROWS, hidden), bf16),
+            pltpu.VMEM((2 * local_experts, EXPERT_ROWS, hidden), bf16),
+            pltpu.VMEM((2, 2, 2, 2, 2, 2, 8, LANES), f32),
+            *[pltpu.VMEM((EXPERT_ROWS, hidden), f32)] * 3,
+            pltpu.VMEM((local_experts, EXPERT_ROWS, LANES), f32),
+            pltpu.VMEM((EXPERT_ROWS, LANES), f32),
+            pltpu.VMEM((EXPERT_ROWS, 2 * local_experts * hidden), bf16),
+            *[pltpu.VMEM((4, 1, EXPERT_ROWS, w * LANES), bf16) for w in (8, 4, 2, 1)],
+            pltpu.VMEM((1, rows, LANES), bf16),
+            pltpu.VMEM((2, 8, rows), f32),
+            pltpu.VMEM((2, 2, 8, rows), f32),
+            pltpu.SemaphoreType.DMA((4,)),
+            pltpu.SemaphoreType.DMA((5,)),
+            pltpu.SemaphoreType.DMA((3,)),
+            pltpu.SemaphoreType.DMA((2,)),
+            pltpu.SemaphoreType.DMA(()),
+            *[pltpu.SemaphoreType.DMA((4, 18))] * 2,
+            *[pltpu.SemaphoreType.DMA((4, 24))] * 2,
+            *[pltpu.SemaphoreType.DMA((2, 2))] * 2,
+            pltpu.SemaphoreType.DMA((2, 2)),
+            *semaphores(4),
+            *semaphores(112),
+        ],
+        compiler_params=pltpu.CompilerParams(
+            collective_id=collective_id,
+            has_side_effects=True,
+            vmem_limit_bytes=60 * 2**20,
+        ),
+    )(attended, wo, x_block, gain, grads_all, w_gate, w_up, w_down, router, mask)
+
+
+def spread_lines(lines, target):
+    for n in range(lines.shape[0]):
+        target[pl.ds(n * LANES, LANES)] = jnp.broadcast_to(lines[n : n + 1], (LANES, LANES)).T
+
+
+def row_lines(values):
+    return jnp.concatenate(
+        [
+            jnp.sum(values[n * LANES : (n + 1) * LANES].T, axis=0, keepdims=True)
+            for n in range(values.shape[0] // LANES)
+        ],
+        axis=0,
+    )
+
+
+def masked_softmax(queries, keys, valid, score_scale):
+    count = queries.shape[0]
+    scores = contract_cols(queries, keys) * score_scale
+    line = lax.broadcasted_iota(jnp.int32, (count, count), 0)
+    lane = lax.broadcasted_iota(jnp.int32, (count, count), 1)
+    scores = jnp.where(jnp.logical_and(lane <= line, valid > 0.5), scores, NEGATIVE)
+    weights = jnp.exp(scores - jnp.max(scores, axis=1, keepdims=True))
+    return weights / jnp.sum(weights, axis=1, keepdims=True)
+
+
+def attend_kernel(
+    width, query_pre, key_pre, values, tables, key_valid, gains,
+    queries, keys, attended, scales,
+    squares, parts, column, send, recv,
+):
+    bits = place_bits()
+    rank = 8 * bits["z"] + 4 * bits["x"] + 2 * bits["y"] + bits["c"]
+    wires = Wires(bits, send, recv)
+    rows = query_pre.shape[0]
+    count = rows // 2
+    for n, pre in enumerate((query_pre, key_pre)):
+        squares[n] = row_lines(pre[...] * pre[...])
+    greet(bits, CUBE_MASKS)
+    copies = [wires.start(squares, parts.at[rank], *names) for names in CUBE_MASKS]
+    parts[rank] = squares[...]
+    receive(copies)
+    scales[...] = lax.rsqrt(jnp.sum(parts[...], axis=0) / width + EPSILON)
+    for n, (pre, target) in enumerate(((query_pre, queries), (key_pre, keys))):
+        spread_lines(scales[n], column)
+        for s in (0, 1):
+            at = pl.ds(s * count, count)
+            normed = pre[at] * column[at] * gains[n : n + 1]
+            turned = normed * tables[0] + pltpu.roll(normed, HEAD_DIM // 2, 1) * tables[1]
+            target[at] = turned.astype(jnp.bfloat16)
+    for s in (0, 1):
+        at = pl.ds(s * count, count)
+        probability = masked_softmax(
+            queries[at], keys[at], key_valid[s : s + 1], HEAD_DIM ** (-0.5)
+        )
+        attended[at] = jnp.dot(
+            probability.astype(jnp.bfloat16), values[at], preferred_element_type=jnp.float32
+        ).astype(jnp.bfloat16)
+    wires.finish()
+
+
+def attend(query_pre, key_pre, values, tables, key_valid, gains, width, collective_id):
+    rows = query_pre.shape[0]
+    column = jax.ShapeDtypeStruct((rows, LANES), jnp.bfloat16)
+    lines = (2, rows // LANES, LANES)
+
+    def kernel(*refs):
+        attend_kernel(width, *refs)
+
+    return pl.pallas_call(
+        kernel,
+        out_shape=(column, column, column, jax.ShapeDtypeStruct(lines, jnp.float32)),
+        in_specs=[IN_VMEM] * 6,
+        out_specs=[IN_VMEM] * 4,
+        scratch_shapes=[
+            pltpu.VMEM(lines, jnp.float32),
+            pltpu.VMEM((16,) + lines, jnp.float32),
+            pltpu.VMEM((rows, LANES), jnp.float32),
+            *semaphores(16),
+        ],
+        compiler_params=pltpu.CompilerParams(
+            collective_id=collective_id, has_side_effects=True, vmem_limit_bytes=32 * 2**20
+        ),
+    )(query_pre, key_pre, values, tables, key_valid, gains)
+
+
+def attend_sequence_back(queries, keys, values, grads, valid, score_scale):
+    probability = masked_softmax(queries, keys, valid, score_scale)
+    prob_grad = contract_cols(grads, values)
+    centre = jnp.sum(probability * prob_grad, axis=1, keepdims=True)
+    score_grad = (probability * (prob_grad - centre)).astype(jnp.bfloat16)
+    query_grad = jnp.dot(score_grad, keys, preferred_element_type=jnp.float32) * score_scale
+    key_grad = rows_dot(score_grad, queries) * score_scale
+    value_grad = rows_dot(probability.astype(jnp.bfloat16), grads)
+    return query_grad, key_grad, value_grad
+
+
+def turn_back(values, cosine, sine_signed):
+    return values * cosine - pltpu.roll(values, HEAD_DIM // 2, 1) * sine_signed
+
+
+def backward_kernel(
+    low, out_part, normed_in, heads_in, head_output_in,
+    middle_grad, queries, keys, values, attended, query_pre, key_pre,
+    x_block, row_values, tables, key_valid, gains, pack_in,
+    arrived, out_rows, grad_rows, packs,
+    low_all, normed, heads, head_output, query_scale, key_scale, scale_in, row_valid, part, pieces, left, query_norm, key_norm, inner, pack,
+    out_block, grad_block, squares, square_parts, terms, term_parts, cross,
+    *scratch,
+):
+    out_pool, part_pool = scratch[:8], scratch[8:16]
+    out_local, part_local, load, own_piece, send, recv = scratch[16:]
+    bits = place_bits()
+    h, z, x, y, c = (bits[n] for n in "hzxyc")
+    ep = 4 * h + 2 * z + x
+    rows, width = low_all.shape
+    count = rows // 2
+    score_scale = HEAD_DIM ** (-0.5)
+    f32, bf16 = jnp.float32, jnp.bfloat16
+    wires = Wires(bits, send, recv)
+    rank = 8 * z + 4 * x + 2 * y + c
+    [(offset, _)] = held_segments(bits, (), BLOCK_BITS)
+    own_cols = pl.ds(offset, LANES)
+
+    own = pltpu.make_async_copy(low, low_all.at[:, own_cols], load.at[0])
+    own.start()
+    loads = [
+        pltpu.make_async_copy(heads_in, heads, load.at[1]),
+        pltpu.make_async_copy(normed_in, normed, load.at[2]),
+        pltpu.make_async_copy(head_output_in, head_output, load.at[3]),
+    ]
+    for copy in loads:
+        copy.start()
+    greet(bits, [*CUBE_MASKS, *[names for names in EP_MASKS if "h" in names]])
+
+    cuts = row_cuts(rows)
+    arriving = [[] for _ in cuts]
+    gathered = [()] * len(cuts)
+
+    def low_stage(stage):
+        for k, (lo, n, turns) in enumerate(cuts):
+            receive(arriving[k])
+            arriving[k] = start_stage(
+                wires, bits, BLOCK_BITS, low, low_all, (), lo, n, gathered[k], turns[stage]
+            )
+            gathered[k] = gathered[k] + (turns[stage],)
+
+    low_stage(0)
+    outs = reductions(
+        wires,
+        bits,
+        out_pool,
+        out_local,
+        [
+            (out_part.at[h if side == 0 else 1 - h, pl.ds(lo, STRIP)], (side, lo))
+            for side in (1, 0)
+            for lo in range(0, rows, STRIP)
+        ],
+    )
+
+    def out_stage(stage):
+        for chunk in outs:
+            chunk.step(stage)
+            side, lo = chunk.what
+            if stage == 4 and side == 1:
+                chunk.copies = [
+                    wires.start(chunk.buffers["a"][3], cross.at[pl.ds(lo, STRIP)], "h")
+                ]
+
+    own.wait()
+    low_stage(1)
+    for n, target in enumerate((query_scale, key_scale, scale_in, row_valid)):
+        spread_lines(row_values[n], target)
+    low_stage(2)
+    out_stage(1)
+    low_stage(3)
+    for copies in arriving:
+        receive(copies)
+    for copy in loads:
+        copy.wait()
+
+    half = HEAD_DIM
+    for s in (0, 1):
+        at = pl.ds(s * count, count)
+        attended_grad = jnp.dot(
+            low_all[at], head_output[...], preferred_element_type=f32
+        ).astype(bf16)
+        query_grad, key_grad, value_grad = attend_sequence_back(
+            queries[at], keys[at], values[at], attended_grad, key_valid[s : s + 1], score_scale
+        )
+        query_norm[at] = turn_back(query_grad, tables[0], tables[1])
+        key_norm[at] = turn_back(key_grad, tables[0], tables[1])
+        left[at, 2 * half :] = value_grad.astype(bf16)
+        lines = pl.ds(s * (count // LANES), count // LANES)
+        squares[0, lines] = row_lines(gains[0:1] * query_norm[at] * query_pre[at])
+        squares[1, lines] = row_lines(gains[1:2] * key_norm[at] * key_pre[at])
+    inner_copies = [wires.start(squares, square_parts.at[rank], *names) for names in CUBE_MASKS]
+    square_parts[rank] = squares[...]
+
+    piece_copies = []
+
+    own_head = pl.ds(pl.multiple_of((2 * z + x) * half, half), half)
+    own_pieces = []
+
+    def send_pieces(m):
+        cols = pl.ds(m * half, half)
+        mine = pltpu.make_async_copy(
+            pieces.at[ep, :, cols], arrived.at[h, m, :, own_head], own_piece.at[m]
+        )
+        mine.start()
+        own_pieces.append(mine)
+        for names in sorted(EP_MASKS, key=lambda names: "h" not in names):
+            to = [1 - bits[n] if n in names else bits[n] for n in "hzx"]
+            piece_copies.append(
+                wires.start(
+                    pieces.at[4 * to[0] + 2 * to[1] + to[2], :, cols],
+                    arrived.at[h, m, :, own_head],
+                    *names,
+                )
+            )
+
+    def add_pieces(source, right, columns):
+        rows_of = pieces.shape[1]
+
+        @pl.loop(0, 8)
+        def _(n):
+            at = pl.ds(pl.multiple_of(n * rows_of, rows_of), rows_of)
+            pieces[n, :, columns] = rows_dot(source[:, at], right).astype(bf16)
+
+    add_pieces(low_all, attended[...], pl.ds(3 * half, half))
+    send_pieces(3)
+    add_pieces(normed, left[:, 2 * half :], pl.ds(2 * half, half))
+    send_pieces(2)
+    out_stage(2)
+    receive(inner_copies)
+    totals = jnp.sum(square_parts[...], axis=0)
+    for n, (pre, norm, scale) in enumerate(
+        ((query_pre, query_norm, query_scale), (key_pre, key_norm, key_scale))
+    ):
+        spread_lines(totals[n], inner)
+        value = scale[...]
+        left[:, pl.ds(n * half, half)] = (
+            value * gains[n : n + 1] * norm[...]
+            - pre[...] * value * value * value * inner[...] / width
+        ).astype(bf16)
+        pack[pl.ds(16 + 2 + n, 1)] = jnp.sum(norm[...] * pre[...] * value, axis=0, keepdims=True)
+    terms[...] = row_lines(
+        left[:, :half].astype(f32) * query_pre[...]
+        + left[:, half : 2 * half].astype(f32) * key_pre[...]
+        + left[:, 2 * half :].astype(f32) * values[...].astype(f32)
+    )
+    term_copies = [wires.start(terms, term_parts.at[rank], *names) for names in CUBE_MASKS]
+    term_parts[rank] = terms[...]
+
+    tile = 512
+
+    @pl.loop(0, width // tile)
+    def _(t):
+        at = pl.ds(pl.multiple_of(t * tile, tile), tile)
+        part[:, at] = contract_cols(left[...], heads[at]).astype(bf16)
+
+    sums = reductions(
+        wires, bits, part_pool, part_local,
+        [(part.at[pl.ds(lo, STRIP)], lo) for lo in range(0, rows, STRIP)],
+    )
+    add_pieces(normed, left[:, : 2 * half], pl.ds(0, 2 * half))
+    send_pieces(0)
+    send_pieces(1)
+    for chunk in sums:
+        chunk.step(1)
+    out_stage(3)
+    for chunk in sums:
+        chunk.step(2)
+    out_stage(4)
+    for chunk in sums:
+        chunk.step(3)
+
+    seg = rows // 16
+    first, own_rows = [], []
+
+    def send_rows(block, whole):
+        def rows_for(owner):
+            return block.at[:, pl.ds(pl.multiple_of(owner * seg, seg), seg)]
+
+        target = whole.at[h, :, :, own_cols]
+        mine = pltpu.make_async_copy(rows_for(ep), target, load.at[1 + len(own_rows)])
+        mine.start()
+        own_rows.append(mine)
+        for names in sorted(EP_MASKS, key=lambda names: "h" not in names):
+            to = [1 - bits[n] if n in names else bits[n] for n in "hzx"]
+            first.append(wires.start(rows_for(4 * to[0] + 2 * to[1] + to[2]), target, *names))
+
+    for chunk in outs:
+        side, lo = chunk.what
+        if side == 1:
+            receive(chunk.copies)
+    for chunk in outs:
+        side, lo = chunk.what
+        if side == 0:
+            at = pl.ds(lo, STRIP)
+            total = chunk.buffers["a"][3][...].astype(f32) + cross[at].astype(f32)
+            out_block[lo // count, pl.ds(lo % count, STRIP)] = (total * row_valid[at]).astype(bf16)
+    send_rows(out_block, out_rows)
+    receive(term_copies)
+    spread_lines(jnp.sum(term_parts[...], axis=0), inner)
+    for chunk in sums:
+        chunk.step(4)
+    for chunk in sums:
+        lo = chunk.what
+        at = pl.ds(lo, STRIP)
+        normed_grad = chunk.buffers["a"][3][...].astype(f32)
+        scale, own_x = scale_in[at], x_block[at].astype(f32)
+        grad_block[lo // count, pl.ds(lo % count, STRIP)] = (
+            middle_grad[at]
+            + scale * gains[2:3] * normed_grad
+            - own_x * (scale * scale * inner[at] / width)
+        ).astype(bf16)
+        query_norm[at] = normed_grad * own_x * scale
+    send_rows(grad_block, grad_rows)
+    pack[pl.ds(0, 16)] = pack_in[pl.ds(0, 16)]
+    pack[pl.ds(16, 1)] = jnp.sum(query_norm[...], axis=0, keepdims=True)
+    pack[pl.ds(17, 1)] = pack_in[pl.ds(17, 1)]
+    pack[pl.ds(20, 4)] = jnp.zeros((4, LANES), f32)
+    packs[h, :, own_cols] = pack[...]
+    for names in EP_MASKS:
+        first.append(wires.start(pack, packs.at[h, :, own_cols], *names))
+    receive(first)
+    for copy in own_rows:
+        copy.wait()
+    gathered = ("z", "x")
+    for name in "yc":
+        copies = []
+        for at, wide in held_segments(bits, gathered, BLOCK_BITS):
+            cols = pl.ds(at, wide)
+            for segment in (
+                out_rows.at[:, :, :, cols], grad_rows.at[:, :, :, cols], packs.at[:, :, cols]
+            ):
+                copies.append(wires.start(segment, segment, name))
+        receive(copies)
+        gathered += (name,)
+    receive(piece_copies)
+    for copy in own_pieces:
+        copy.wait()
+    wires.finish()
+
+
+def run_backward(low, out_part, normed_in, heads, head_output, vectors, collective_id):
+    f32, bf16 = jnp.float32, jnp.bfloat16
+    rows, width = normed_in.shape
+    chunks = rows // STRIP
+    column = (rows, LANES)
+    lines = (rows // LANES, LANES)
+    ep_count = 8
+    return pl.pallas_call(
+        backward_kernel,
+        out_shape=(
+            jax.ShapeDtypeStruct((2, 4, width // ep_count, 4 * LANES), bf16),
+            jax.ShapeDtypeStruct((2, 2, rows // 16, width), bf16),
+            jax.ShapeDtypeStruct((2, 2, rows // 16, width), bf16),
+            jax.ShapeDtypeStruct((2, 24, width), f32),
+        ),
+        in_specs=[ANYWHERE] * 5 + [IN_VMEM] * len(vectors),
+        out_specs=[ANYWHERE] * 3 + [IN_VMEM],
+        scratch_shapes=[
+            pltpu.VMEM((rows, width), bf16),
+            pltpu.VMEM((rows, width), bf16),
+            pltpu.VMEM(heads.shape, bf16),
+            pltpu.VMEM(head_output.shape, bf16),
+            *[pltpu.VMEM(column, f32)] * 4,
+            pltpu.VMEM((rows, width), bf16),
+            pltpu.VMEM((ep_count, width // ep_count, 4 * LANES), bf16),
+            pltpu.VMEM((rows, 3 * LANES), bf16),
+            pltpu.VMEM(column, f32),
+            pltpu.VMEM(column, f32),
+            pltpu.VMEM(column, f32),
+            pltpu.VMEM((24, LANES), f32),
+            pltpu.VMEM((2, rows // 2, LANES), bf16),
+            pltpu.VMEM((2, rows // 2, LANES), bf16),
+            pltpu.VMEM((2,) + lines, f32),
+            pltpu.VMEM((16, 2) + lines, f32),
+            pltpu.VMEM(lines, f32),
+            pltpu.VMEM((16,) + lines, f32),
+            pltpu.VMEM(column, bf16),
+            *reduction_buffers(2 * chunks, STRIP),
+            *reduction_buffers(chunks, STRIP),
+            pltpu.SemaphoreType.DMA((2 * chunks,)),
+            pltpu.SemaphoreType.DMA((chunks,)),
+            pltpu.SemaphoreType.DMA((5,)),
+            pltpu.SemaphoreType.DMA((4,)),
+            *semaphores(288),
+        ],
+        compiler_params=pltpu.CompilerParams(
+            collective_id=collective_id,
+            has_side_effects=True,
+            vmem_limit_bytes=60 * 2**20,
+        ),
+    )(low, out_part, normed_in, heads, head_output, *vectors)
+
+
+def column_block(values, index, width=LANES):
+    return lax.dynamic_slice_in_dim(values, index * width, width, axis=-1)
+
+
+def as_tiles(values):
+    return values.reshape(values.shape[:-1] + (values.shape[-1] // LANES, LANES))
+
+
+def cube_shards(
+    inputs,
+    lengths,
+    routes,
+    w_query,
+    w_key,
+    w_value,
+    w_output,
+    w_router,
+    attn_gain,
+    moe_gain,
+    query_gain,
+    key_gain,
+    w_gate,
+    w_up,
+    w_down,
+    out_grad,
+):
+    f32, bf16 = jnp.float32, jnp.bfloat16
+    micro_count, block_rows, sequence_count, width = inputs.shape
+    ep_index = lax.axis_index("ep")
+    ep_count = lax.axis_size("ep")
+    local_experts = w_gate.shape[0]
+    hidden = w_gate.shape[2]
+    expert_count = local_experts * ep_count
+    rows_dev = block_rows * sequence_count
+    sequence_length = block_rows * ep_count
+    rows = rows_dev * ep_count
+    bits = place_bits()
+    micro = bits["h"]
+    block = block_index(bits, BLOCK_BITS)
+    head = block_index(bits, HEAD_BITS)
+
+    named = routes.transpose(0, 2, 1, 3).reshape(micro_count * rows_dev, -1)
+    expert_numbers = jnp.arange(expert_count, dtype=jnp.int32)
+    mask_own = jnp.any(named[:, :, None] == expert_numbers, axis=1).astype(bf16)
+    small = jnp.concatenate(
+        [
+            w_router.T,
+            jnp.concatenate([attn_gain, moe_gain, query_gain, key_gain]).reshape(4, -1),
+            mask_own.T,
+            jnp.zeros((40 - 4 - 2 * expert_count, w_router.shape[0]), bf16),
+        ],
+        axis=0,
+    )
+    local_place = ep_index * block_rows + jnp.arange(block_rows, dtype=jnp.int32)
+    quarter = block_rows // lax.axis_size("tp")
+    tp_index = lax.axis_index("tp")
+    grad_quarter = lax.dynamic_slice_in_dim(out_grad, tp_index * quarter, quarter, axis=1)
+    place_quarter = lax.dynamic_slice_in_dim(local_place, tp_index * quarter, quarter)
+    valid_quarter = (place_quarter[None, :, None] < lengths[:, None, :]).astype(bf16)
+    grad_quarter = (grad_quarter * valid_quarter[..., None]).transpose(0, 2, 1, 3)
+    g_all = lax.all_gather(grad_quarter, ("ep", "tp"))
+    x_all, w_heads, small_all = spread_inputs(
+        inputs.transpose(0, 2, 1, 3).reshape(micro_count, rows_dev, width),
+        w_query,
+        w_key,
+        w_value,
+        small,
+    )
+    router = small_all[:, :expert_count].transpose(0, 2, 1).reshape(width, expert_count)
+    gains = small_all[:, expert_count : expert_count + 4].transpose(1, 0, 2).reshape(4, width)
+    gains = gains.astype(f32)
+    gain_attn = gains[0]
+    gain_moe = column_block(gains[1], block)
+    gain_query = column_block(gains[2], head)
+    gain_key = column_block(gains[3], head)
+    mask = small_all[:, expert_count + 4 : 2 * expert_count + 4]
+    mask = mask.reshape(ep_count, expert_count, micro_count, sequence_count, block_rows)
+    mask = mask.transpose(2, 3, 0, 4, 1).reshape(micro_count * rows, expert_count).astype(f32)
+    lengths_own = lax.dynamic_index_in_dim(lengths, micro, keepdims=False)
+
+    x_float = x_all.astype(f32)
+    scale_in = row_scale(x_float)
+    normed_in = lax.optimization_barrier((x_float * scale_in * gain_attn).astype(bf16))
+    projected = jnp.dot(normed_in, w_heads, preferred_element_type=f32)
+    query_pre = projected[:, :LANES]
+    key_pre = projected[:, LANES : 2 * LANES]
+    value_rows = projected[:, 2 * LANES :].astype(bf16)
+    places = np.arange(sequence_length, dtype=np.float32)
+    inverse = np.float32(THETA_BASE) ** (
+        -np.arange(HEAD_DIM // 2, dtype=np.float32) * np.float32(2.0 / HEAD_DIM)
+    )
+    angles = places[:, None] * inverse[None, :]
+    sines = np.sin(angles)
+    tables = jnp.asarray(
+        np.stack(
+            [
+                np.concatenate([np.cos(angles)] * 2, axis=1),
+                np.concatenate([-sines, sines], axis=1),
+            ]
+        )
+    )
+    valid_rows = (jnp.arange(sequence_length) < lengths_own[:, None]).astype(f32)
+    gains_block = jnp.stack([gain_query, gain_key, column_block(gain_attn, block)])
+    queries, keys, attended, scales = attend(
+        query_pre, key_pre, value_rows, tables, valid_rows, gains_block, width, 1
+    )
+    x_block = column_block(x_all, block)
+
+    pad = ((0, 0), (0, LANES - expert_count))
+    mask = jnp.pad(mask, pad).astype(bf16).reshape(micro_count, rows, LANES)
+    (
+        middle,
+        middle_gained,
+        w_head_output,
+        out_part,
+        normed_grad_block,
+        tiny_all,
+        logits,
+        grad_gate,
+        grad_up,
+        grad_down,
+    ) = run_experts(
+        attended,
+        w_output,
+        x_block,
+        gain_moe[None],
+        g_all,
+        w_gate,
+        w_up,
+        w_down,
+        jnp.pad(router, pad),
+        mask,
+        3,
+    )
+    w_head_output = w_head_output.reshape(width, LANES)
+    tiny_all = tiny_all.reshape(ep_count, 8, rows)
+    gate_grad_rows = tiny_all[:, :local_experts].reshape(expert_count, rows).T
+    row_terms = jnp.sum(tiny_all[:, local_experts], axis=0)[:, None]
+
+    def own_micro(values):
+        return lax.dynamic_index_in_dim(values, micro, keepdims=False)
+
+    logits_own = logits
+    scale_own = logits_own[:, expert_count : expert_count + 1]
+    logits_own = logits_own[:, :expert_count]
+    mask_rows = own_micro(mask)[:, :expert_count].astype(f32)
+    probs_own = jax.nn.softmax(logits_own, axis=-1)
+    prob_grad = gate_grad_rows * mask_rows
+    logit_grad = (
+        probs_own * (prob_grad - jnp.sum(probs_own * prob_grad, axis=1, keepdims=True))
+    ).astype(bf16)
+    router_block = lax.dynamic_slice_in_dim(router, block * LANES, LANES, axis=0)
+    logit_grad_float = logit_grad.astype(f32)
+    row_terms = row_terms + jnp.sum(logit_grad_float * logits_own, axis=1, keepdims=True)
+    grad_router_part = contract_rows(
+        (logit_grad_float * scale_own).astype(bf16), middle_gained
+    )
+    normed_grad_block = normed_grad_block + scale_own * contract_cols(logit_grad, router_block)
+    grad_block = lax.dynamic_index_in_dim(column_block(g_all, block), micro, axis=1, keepdims=False)
+    grad_block = grad_block.transpose(1, 0, 2, 3).reshape(rows, LANES).astype(f32)
+    middle_grad = (
+        grad_block
+        + gain_moe * normed_grad_block
+        - middle * (scale_own * scale_own * row_terms / width)
+    )
+    grad_gain_moe = jnp.sum(normed_grad_block * middle, axis=0)
+    pack = jnp.concatenate(
+        [
+            grad_router_part,
+            jnp.zeros((1, LANES), f32),
+            grad_gain_moe[None],
+            jnp.zeros((24 - 2 - expert_count, LANES), f32),
+        ],
+        axis=0,
+    )
+
+    grad_pieces, out_rows, input_grad_rows, packs = run_backward(
+        middle_grad.astype(bf16),
+        out_part,
+        normed_in,
+        w_heads,
+        w_head_output,
+        [
+            middle_grad,
+            queries,
+            keys,
+            value_rows,
+            attended,
+            query_pre,
+            key_pre,
+            x_block,
+            jnp.stack(
+                [
+                    scales[0],
+                    scales[1],
+                    as_tiles(scale_in[:, 0]),
+                    as_tiles(valid_rows.reshape(rows)),
+                ]
+            ),
+            tables,
+            valid_rows,
+            gains_block,
+            pack,
+        ],
+        5,
+    )
+    packs = jnp.sum(packs, axis=0)
+    own_block = column_block(packs, ep_index, width // ep_count)
+    head_rows = packs[expert_count + 2 : expert_count + 4].reshape(2, 2, 2, 2, 2, LANES)
+    head_rows = head_rows.transpose(0, 4, 1, 2, 3, 5).reshape(2, width)
+    own_head = column_block(head_rows, ep_index, width // ep_count)
+    weight_grads = [
+        grad_pieces[0, m].astype(f32) + grad_pieces[1, m].astype(f32) for m in range(4)
+    ]
+    return (
+        out_rows.transpose(0, 2, 1, 3),
+        input_grad_rows.transpose(0, 2, 1, 3).astype(f32),
+        *weight_grads,
+        own_block[:expert_count].T,
+        own_block[expert_count],
+        own_block[expert_count + 1],
+        own_head[0],
+        own_head[1],
+        grad_gate,
+        grad_up,
+        grad_down,
+    )
+
+
+def shards(inputs, lengths, routes, *rest):
+    sizes = (lax.axis_size("ep"), lax.axis_size("tp"), inputs.shape[0])
+    local_heads = rest[0].shape[1] // HEAD_DIM
+    if sizes == (8, 4, 2) and local_heads == 4:
+        return cube_shards(inputs, lengths, routes, *rest)
+    return routed_shards(inputs, lengths, routes, *rest)
 
 
 def solution(mesh):

time: 2380 us -> 488 us (0.21)
  waiting for transfers between devices: 1610 us -> 0.04 us
  Pallas kernels: 0 us -> 403 us
  local copies, waits for them, and re-layouts: 227 us -> 32.4 us
  blocking collectives: 154 us -> 0 us
  matrix products: 151 us -> 3.94 us
  other arithmetic: 163 us -> 23.5 us
  starting transfers between devices: 46.6 us -> 0.04 us
    all_to_all x8 -> x0, waiting for transfers between devices: 990 us -> none  [the longest x2 394 us: shards(): lax.all_to_all(expert_grad, 'ep', split_axis=0, concat_axis=0, tiled=True)]
    pallas_call x0 -> x4, Pallas kernels: none -> 403 us  [the longest x1 164 us: run_experts(): pl.pallas_call(experts_kernel, out_shape=(jax.ShapeDtypeStruct((rows, LAN...]
    reduce_scatter x7 -> x0, waiting for transfers between devices: 298 us -> none  [the longest x2 80.1 us: shards(): lax.psum_scatter(key_grad_all.astype(jnp.bfloat16), 'ep', scatter_dimensi...]
    all_gather x8 -> x1, waiting for transfers between devices: 120 us -> 0.02 us  [cube_shards(): g_all = lax.all_gather(grad_quarter, ('ep', 'tp'))]
    dot_general x52 -> x1, matrix products: 122 us -> 2.32 us  [cube_shards(): projected = jnp.dot(normed_in, w_heads, preferred_element_type=f32)]
    unnamed x20 -> x1, waiting for transfers between devices: 102 us -> 0.02 us
    psum x3 -> x0, waiting for transfers between devices: 97.7 us -> none  [the longest x1 48.7 us: shards(): attn_rows = lax.psum(contract_cols(attended, full_output), 'tp')]
    all_gather x5 -> x0, blocking collectives: 84 us -> none  [the longest x1 25.2 us: shards(): lax.all_gather(w_router, 'ep', axis=0, tiled=True)]
  transfers between devices with their start and end apart: 27 -> 1, of which waited for: 23 -> 0; matrix products, arithmetic and copies ran while one was open for 20% -> 4% of each run, Pallas kernels for 0% -> 20%
where the time goes in v1:
time: 488 us; the launch traced here: 478 us
  Pallas kernels  403 us (83%)
  local copies, waits for them, and re-layouts  32.4 us (7%)
  other arithmetic  23.5 us (5%)
  between operations  15.2 us (3%)
    pallas_call x1, Pallas kernels, run_experts(): pl.pallas_call(experts_kernel, out_shape=(jax.ShapeDtypeStruct((rows, LAN...  164 us
    pallas_call x1, Pallas kernels, run_backward(): pl.pallas_call(backward_kernel, out_shape=(jax.ShapeDtypeStruct((2, 4, wi...  145 us
    pallas_call x1, Pallas kernels, spread_inputs(): pl.pallas_call(spread_kernel, out_shape=(jax.ShapeDtypeStruct((2, 2, 2, 2...  80.6 us
    unnamed x64, local copies, waits for them, and re-layouts  19.8 us
    pallas_call x1, Pallas kernels, attend(): pl.pallas_call(kernel, out_shape=(column, column, column, jax.ShapeDtypeS...  13 us
  transfers between devices with their start and end apart: 1, of which 0 were waited for; matrix products, arithmetic and copies ran while one was open for 4% of the time, Pallas kernels for 20%

profile of v1, /device:TPU:1, one launch (start us, length us, event | category | flops | bytes accessed | tf_op | source)
XLA Modules:
  0.0 478.2 jit_solution(11758084840001979287)
XLA Ops:
  7.3 1.2 copy-done
  8.7 0.8 compare_convert_fusion.1
  9.4 0.8 fusion.8
  10.3 2.5 copy.80
  14.5 1.4 maximum_maximum_fusion.small
  15.9 80.6 %shard_map.272 = (bf16[2,2,2,2,2,32,2048]{6,5,4,3,2,1,0:T(8,128)(2,1)}, bf16[2,2,2,256,384]{4,3,2,1,0:T(8,128)(2,1)}, bf16[2,2,2,40,256]{4,3,2,1,0:T(8,128)(2,1)}) custom-call(bf16[2,2,2,32,2048]{4,3,2,1,0:T(8,128)(2,1)} %bitcast.98, bf16[256,512]{1,0:T(8,128)(2,1)} %wq.1, bf16[256,512]{1,0:T(8,128)(2,1)} %wk.1, bf16[256,512]{1,0:T(8,128)(2,1)} %wv.1, ...), custom_call_target="tpu_custom_call" | custom-call | tf_op jit(solution)/shard_map/pallas_call | solution.py:684
  96.6 3.1 multiply_reduce_fusion
  100.0 3.3 multiply_convert_fusion.normed_in
  103.3 2.3 fusion.21
  105.8 1.0 copy-done.18
  107.1 0.9 pad.9.router_in
  109.5 1.3 fusion.17
  110.8 13.0 %shard_map.273 = (bf16[1024,128]{1,0:T(8,128)(2,1)S(1)}, bf16[1024,128]{1,0:T(8,128)(2,1)S(1)}, bf16[1024,128]{1,0:T(8,128)(2,1)S(1)}, f32[2,8,128]{2,1,0:T(8,128)S(1)}) custom-call(f32[1024,128]{1,0:T(8,128)S(1)} %get-tuple-element.137.refs_0_.query_pre, f32[1024,128]{1,0:T(8,128)S(1)} %get-tuple-element.136.refs_1_.key_pre, ...), custom_call_target="tpu_custom_call" | custom-call | tf_op jit(solution)/shard_map/pallas_call | solution.py:1487
  125.3 1.7 constant_dynamic-slice_fusion.1.x_block
  127.0 164.5 %shard_map.274 = (f32[1024,128]{1,0:T(8,128)}, bf16[1024,128]{1,0:T(8,128)(2,1)}, bf16[2,2,2,256,128]{4,3,2,1,0:T(8,128)(2,1)}, bf16[2,1024,2048]{2,1,0:T(8,128)...) custom-call(bf16[1024,128]{1,0:T(8,128)(2,1)} %copy-done.6, ...), custom_call_target="tpu_custom_call" | custom-call | tf_op jit(solution)/shard_map/pallas_call | solution.py:1361
  291.6 1.1 slice_reduce_fusion.2
  292.7 1.0 slice.146
  293.9 1.3 slice_reduce_fusion.1
  295.3 1.4 fusion.5
  296.7 1.5 multiply_reduce_fusion.3
  298.2 1.7 fusion.1
  300.6 1.2 convert_bitcast_fusion.1
  302.3 1.3 fusion.15
  304.2 145.0 %shard_map.275 = (bf16[2,4,256,512]{3,2,1,0:T(8,128)(2,1)}, bf16[2,2,64,2048]{3,2,1,0:T(8,128)(2,1)}, bf16[2,2,64,2048]{3,2,1,0:T(8,128)(2,1)}, f32[2,24,2048]{2,1,0:T(8,128)}) custom-call(bf16[1024,128]{1,0:T(8,128)(2,1)} %get-tuple-element.128.low, bf16[2,1024,2048]{2,1,0:T(8,128)(2,1)} %get-tuple-element.43.out_part, bf16[1024,2048]{1,0:T(8,128)(2,1)} %copy-done.11, ...), custom_call_target="tpu_custom_call" | custom-call | tf_op jit(solution)/shard_map/pallas_call | solution.py:1771
  449.2 3.3 copy.89
  452.5 1.6 convert_bitcast_fusion
  454.1 2.9 copy.90
  457.0 1.4 add_bitcast_fusion
  460.5 4.6 copy.108
  465.2 2.1 copy.109
  467.3 1.6 copy-done.13
  468.9 2.0 copy.110
  (111 shorter events, 9.6 us)
Async XLA Ops:
  7.2 1.2 copy-start
  7.2 119.8 %all-gather.3.cloned.1.call-start = ((), (), s32[]{:S(2)}) async-start(), calls=%async_computation | async-start | bytes 8650752 | tf_op jit(solution)/shard_map/all_gather | solution.py:1877
  96.6 3.4 copy-start.23
  100.0 3.3 copy-start.17
  103.3 2.4 copy-start.11
  105.7 1.1 copy-start.18
  105.7 2.9 copy-start.25
  105.7 5.1 %copy-start.5 = (f32[2,512,128]{2,1,0:T(8,128)S(1)}, f32[2,512,128]{2,1,0:T(8,128)}, u32[]{:S(2)}) copy-start(f32[2,512,128]{2,1,0:T(8,128)} %constant.135.clone.refs_3_.tables) | copy-start | bytes 1572868
  105.7 21.2 %copy-start.4 = (bf16[1024,128]{1,0:T(8,128)(2,1)}, bf16[1024,128]{1,0:T(8,128)(2,1)S(1)}, u32[]{:S(2)}) copy-start(bf16[1024,128]{1,0:T(8,128)(2,1)S(1)} %slice.177.refs_2_.values) | copy-start | bytes 786436
  108.5 18.5 %copy-start.15 = (bf16[2048,128]{1,0:T(8,128)(2,1)}, bf16[2048,128]{1,0:T(8,128)(2,1)S(1)}, u32[]{:S(2)}) copy-start(bf16[2048,128]{1,0:T(8,128)(2,1)S(1)} %pad.10) | copy-start | bytes 1572868
  109.4 182.1 %copy-start.10 = (f32[3,128]{1,0:T(4,128)}, f32[3,128]{1,0:T(4,128)S(1)}, u32[]{:S(2)}) copy-start(f32[3,128]{1,0:T(4,128)S(1)} %pad_maximum_fusion.2.refs_5_.gains) | copy-start | bytes 4612
  109.5 182.1 %copy-start.9 = (f32[2,512]{1,0:T(2,128)}, f32[2,512]{1,0:T(2,128)S(1)}, u32[]{:S(2)}) copy-start(f32[2,512]{1,0:T(2,128)S(1)} %compare_convert_fusion.refs_4_.key_valid) | copy-start | bytes 12292
  110.8 180.8 %copy-start.2 = (f32[1024,128]{1,0:T(8,128)}, f32[1024,128]{1,0:T(8,128)S(1)}, u32[]{:S(2)}) copy-start(f32[1024,128]{1,0:T(8,128)S(1)} %get-tuple-element.136.refs_1_.key_pre) | copy-start | bytes 1572868
  110.8 180.8 %copy-start.3 = (f32[1024,128]{1,0:T(8,128)}, f32[1024,128]{1,0:T(8,128)S(1)}, u32[]{:S(2)}) copy-start(f32[1024,128]{1,0:T(8,128)S(1)} %get-tuple-element.137.refs_0_.query_pre) | copy-start | bytes 1572868
  123.8 0.7 copy-start.8
  124.5 2.5 copy-start.6
  124.5 2.5 copy-start.7
  291.6 8.6 %copy-start.12 = (f32[1024,128]{1,0:T(8,128)S(1)}, f32[1024,128]{1,0:T(8,128)}, u32[]{:S(2)}) copy-start(f32[1024,128]{1,0:T(8,128)} %get-tuple-element.40) | copy-start | bytes 1572868
  291.6 10.3 %copy-start.22 = (bf16[1024,128]{1,0:T(8,128)(2,1)S(1)}, bf16[1024,128]{1,0:T(8,128)(2,1)}, u32[]{:S(2)}) copy-start(bf16[1024,128]{1,0:T(8,128)(2,1)} %get-tuple-element.48) | copy-start | bytes 786436
  293.7 8.6 %copy-start.19 = (f32[1024,128]{1,0:T(8,128)S(1)}, f32[1024,128]{1,0:T(8,128)}, u32[]{:S(2)}) copy-start(f32[1024,128]{1,0:T(8,128)} %get-tuple-element.42) | copy-start | bytes 1572868
  293.7 8.6 %copy-start.20 = (f32[1024,128]{1,0:T(8,128)S(1)}, f32[1024,128]{1,0:T(8,128)}, u32[]{:S(2)}) copy-start(f32[1024,128]{1,0:T(8,128)} %get-tuple-element.39) | copy-start | bytes 1572868
  293.7 8.6 %copy-start.24 = (f32[1,128]{1,0:T(1,128)S(1)}, f32[1,128]{1,0:T(1,128)}, u32[]{:S(2)}) copy-start(f32[1,128]{1,0:T(1,128)} %get-tuple-element.151.gain) | copy-start | bytes 1540
  452.5 4.6 copy-start.16
  454.1 4.4 copy-start.21
  460.5 4.6 copy-start.14
  465.2 3.7 copy-start.13
  465.2 5.7 %copy-start.1 = (bf16[2,64,2,2048]{3,2,1,0:T(2,128)(2,1)S(1)}, bf16[2,64,2,2048]{3,2,1,0:T(2,128)(2,1)}, u32[]{:S(2)}) copy-start(bf16[2,64,2,2048]{3,2,1,0:T(2,128)(2,1)} %param.32) | copy-start | bytes 3145732
Sparse Core Ops, SparseCore 0:
  11.5 112.5 all-gather.2
